TPU v7x, 256 devices: a whole 4x4x8 slice. The times are simulated.
256 devices in a mesh: req: 16 (over y, x), head: 16 (over z, core).
Axes of the slice: x: 4, y: 4, z: 8, core: 2. Of those that a mesh axis runs over, the one named last changes fastest.
Arguments:
- tokens: bfloat16 [2048, 8192], P('req', 'head'), may hold values from -6 to 6
- prior_state: float32 [32, 256, 64, 256], P('req', 'head'), may hold values from -6 to 6
- conv_inner_state: bfloat16 [32, 3, 16384], P('req', None, 'head'), may hold values from -6 to 6
- conv_group_state: bfloat16 [32, 3, 4096], P('req', None, 'head'), may hold values from -6 to 6
- gate_weight: bfloat16 [8192, 16384], P('req', 'head'), may hold values from -0.0625 to 0.0625
- inner_weight: bfloat16 [8192, 16384], P('req', 'head'), may hold values from -0.0625 to 0.0625
- group_weight: bfloat16 [8192, 4096], P('req', 'head'), may hold values from -0.0625 to 0.0625
- step_weight: bfloat16 [8192, 256], P('req', 'head'), may hold values from -0.0625 to 0.0625
- conv_inner_weight: bfloat16 [4, 16384], P(None, 'head'), may hold values from -3 to 3
- conv_inner_bias: bfloat16 [16384], P('head'), may hold values from -3 to 3
- conv_group_weight: bfloat16 [4, 4096], P(None, 'head'), may hold values from -3 to 3
- conv_group_bias: bfloat16 [4096], P('head'), may hold values from -3 to 3
- step_bias: float32 [256], P('head'), may hold values from -4 to -1
- decay_rate: float32 [256], P('head'), may hold values from 0.05 to 4
- skip_gain: float32 [256], P('head'), may hold values from 0.5 to 1.5
- norm_gain: float32 [16384], P('head'), may hold values from 0.1 to 1.9
- out_weight: bfloat16 [16384, 8192], P('head', 'req'), may hold values from -0.046875 to 0.046875
- parents: int32 [32, 64], P('req'), may hold values from -1 to 62, as said below
- accepted_path: int32 [32, 64], P('req'), may hold values from -1 to 63, as said below
- path_length: int32 [32], P('req'), may hold values from 1 to 64, as said below
- tree_size: int32 [32], P('req'), may hold values from 16 to 64, as said below
Outputs:
- mixed: bfloat16 [2048, 8192], P('req', 'head')
- next_state: float32 [32, 256, 64, 256], P('req', 'head')
Inputs may be any that keep to these rules, and one draw needn't show every extreme that they name: parents[r, 0] = -1 and 0 <= parents[r, i] < i for i >= 1. accepted_path[r, 0 .. path_length - 1] runs from slot 0 to a slot below tree_size, each entry the parent of the next; later entries are -1. path_length[r] is at most tree_size[r]; some request accepts all 64 slots. `tree_size`: some tree fills all 64 slots.
All inputs are finite; a program needn't handle non-finite values.
Results may differ from a plain program's by a relative error of at most 0.017.
Values may be sent and summed in bfloat16 or wider, within the bound.
A program may use at most 192 MiB of HBM per device.

v0:
```python
import jax
import jax.numpy as jnp
from jax import lax
from jax.sharding import PartitionSpec as P

HEAD_DIM = 64
STATE = 256
GROUPS = 8
CONV = 4
INNER = 16384


HIGHEST_PRECISION = lax.Precision.HIGHEST


def shortened(shard):

    def short(part):
        return part.astype(jnp.bfloat16) if part.dtype == jnp.float32 else part

    return jax.tree.map(short, shard)


def from_partner(block, axis, stride):
    count = lax.axis_size(axis)
    route = []
    for low in range(count):
        high = low | 1 << stride
        if high != low and high < count:
            route += [(low, high), (high, low)]
    return lax.ppermute(block, axis, route)


def tree_maps(parents):
    node_count = parents.shape[1]
    positions = jnp.arange(node_count, dtype=jnp.int32)
    parent_map = (parents[:, :, None] == positions[None, None, :]).astype(jnp.float32)
    reach = jnp.eye(node_count, dtype=jnp.float32)[None] + parent_map
    for sweep in range(6):
        reach = jnp.minimum(
            jnp.einsum("rij,rjk->rik", reach, reach, precision=HIGHEST_PRECISION), 1.0
        )
    node_depth = jnp.sum(reach, axis=-1) - 1.0
    return (parent_map, reach, node_depth)


def tree_conv(values, prior_inputs, parent_map, node_depth, taps, offset):
    values = values.astype(jnp.float32)
    prior_inputs = prior_inputs.astype(jnp.float32)
    taps = taps.astype(jnp.float32)
    summed = offset.astype(jnp.float32) + taps[CONV - 1] * values
    ancestor_step = jnp.broadcast_to(
        jnp.eye(parent_map.shape[1], dtype=jnp.float32), parent_map.shape
    )
    slot_index = jnp.arange(CONV - 1, dtype=jnp.float32)
    for lag_index in range(1, CONV):
        ancestor_step = jnp.einsum(
            "rij,rjk->rik", ancestor_step, parent_map, precision=HIGHEST_PRECISION
        )
        earlier = (lag_index > node_depth)[..., None] & (
            slot_index[None, None, :] == CONV - 1 - lag_index + node_depth[..., None]
        )
        lagged = jnp.einsum("rij,rjc->ric", ancestor_step, values, precision=HIGHEST_PRECISION)
        lagged = lagged + jnp.einsum(
            "ris,rsc->ric", earlier.astype(jnp.float32), prior_inputs, precision=HIGHEST_PRECISION
        )
        summed = summed + taps[CONV - 1 - lag_index] * lagged
    return jax.nn.silu(summed)


def make_adder(gathered):

    def add_rows(totals, pieces, start):
        return tuple(
            (jnp.dot(gathered, piece, preferred_element_type=jnp.float32) for piece in pieces)
        )

    return add_rows


def join_halves(mine, partner, upper_half):
    return jnp.where(
        upper_half == 1,
        jnp.concatenate((partner, mine), axis=-1),
        jnp.concatenate((mine, partner), axis=-1),
    )


def on_device(
    tokens,
    prior_state,
    conv_inner_state,
    conv_group_state,
    gate_weight,
    inner_weight,
    group_weight,
    step_weight,
    conv_inner_weight,
    conv_inner_bias,
    conv_group_weight,
    conv_group_bias,
    step_bias,
    decay_rate,
    skip_gain,
    norm_gain,
    out_weight,
    parents,
    accepted_path,
    path_length,
    tree_size,
):
    gathered = lax.all_gather(tokens, "head", axis=1, tiled=True)
    request_count, node_count = parents.shape
    token_rows = gathered.shape[0]
    position = lax.axis_index("head")
    add_rows = make_adder(gathered)
    parent_map, reach, node_depth = tree_maps(parents)
    group_parts = (group_weight, conv_group_weight, conv_group_bias, conv_group_state)
    bit_number = 0
    partner = jax.tree.map(
        lambda part, own: part.astype(own.dtype),
        from_partner(shortened(group_parts), "head", bit_number),
        group_parts,
    )
    upper_half = position >> bit_number & 1
    group_parts = tuple(
        (
            join_halves(mine, other_part, upper_half)
            for mine, other_part in zip(group_parts, partner)
        )
    )
    weights = (gate_weight, inner_weight, group_parts[0], step_weight)
    sums = add_rows(
        tuple((jnp.zeros((token_rows, weight.shape[1]), jnp.float32) for weight in weights)),
        (
            lax.all_gather(weights[0], "req", axis=0, tiled=True),
            lax.all_gather(weights[1], "req", axis=0, tiled=True),
            lax.all_gather(weights[2], "req", axis=0, tiled=True),
            lax.all_gather(weights[3], "req", axis=0, tiled=True),
        ),
        jnp.int32(0),
    )
    gate_raw, inner_raw, group_raw, step_raw = (
        summed.astype(jnp.bfloat16).reshape(request_count, node_count, -1) for summed in sums
    )
    group_values = tree_conv(
        group_raw, group_parts[3], parent_map, node_depth, group_parts[1], group_parts[2]
    )
    channels = tree_conv(
        inner_raw, conv_inner_state, parent_map, node_depth, conv_inner_weight, conv_inner_bias
    )
    heads_local = step_raw.shape[-1]
    heads_x = channels.reshape(request_count, node_count, heads_local, HEAD_DIM)
    b_part = group_values[..., :STATE]
    c_part = group_values[..., STATE:]
    step_size = jax.nn.softplus(step_raw.astype(jnp.float32) + step_bias)
    log_decay = -decay_rate * step_size
    cumulative = jnp.einsum("rij,rjh->rih", reach, log_decay, precision=HIGHEST_PRECISION)
    gap = cumulative[:, :, None, :] - cumulative[:, None, :, :]
    decays = jnp.where(reach[..., None] > 0, jnp.exp(jnp.minimum(gap, 0.0)), 0.0)
    intersection = jnp.einsum("rin,rjn->rij", c_part, b_part, precision=HIGHEST_PRECISION)
    mixing = decays * intersection[..., None] * step_size[:, None, :, :]
    output = jnp.einsum("rijh,rjhp->rihp", mixing, heads_x, precision=HIGHEST_PRECISION)
    output = output + jnp.exp(cumulative)[..., None] * jnp.einsum(
        "rin,rhpn->rihp", c_part, prior_state, precision=HIGHEST_PRECISION
    )
    output = output + skip_gain[None, None, :, None] * heads_x
    slot_ids = jnp.arange(node_count, dtype=jnp.int32)
    valid = slot_ids[None, :] < tree_size[:, None]
    output = jnp.where(valid[:, :, None, None], output, 0.0).reshape(request_count, node_count, -1)
    gated = output * jax.nn.silu(gate_raw.astype(jnp.float32))
    squares = jnp.sum(gated * gated, axis=-1)
    bit_number = 0
    squares = squares + from_partner(squares, "head", bit_number)
    mean_square = squares / (INNER // GROUPS)
    normed = (gated * lax.rsqrt(mean_square + 1e-05)[..., None] * norm_gain).astype(jnp.bfloat16)
    normed_flat = normed.reshape(token_rows, -1)
    terms = jnp.dot(
        normed_flat,
        lax.all_gather(out_weight, "req", axis=1, tiled=True),
        preferred_element_type=jnp.float32,
    )
    mixed = lax.psum_scatter(terms, "head", scatter_dimension=1, tiled=True).astype(jnp.bfloat16)
    last_pick = slot_ids[None, :] == (path_length - 1)[:, None]
    leaf_node = jnp.sum(jnp.where(last_pick, accepted_path, 0), axis=1)
    leaf_row = (slot_ids[None, :] == leaf_node[:, None]).astype(jnp.float32)
    leaf_reach = jnp.einsum("ri,rij->rj", leaf_row, reach, precision=HIGHEST_PRECISION)
    leaf_cumulative = jnp.einsum("ri,rih->rh", leaf_row, cumulative, precision=HIGHEST_PRECISION)
    leaf_gap = leaf_cumulative[:, None, :] - cumulative
    weights_leaf = (
        jnp.where(leaf_reach[..., None] > 0, jnp.exp(jnp.minimum(leaf_gap, 0.0)), 0.0) * step_size
    )
    next_state = jnp.exp(leaf_cumulative)[:, :, None, None] * prior_state
    next_state = next_state + jnp.einsum(
        "rjh,rjhp,rjn->rhpn", weights_leaf, heads_x, b_part, precision=HIGHEST_PRECISION
    )
    return (mixed, next_state)


def solution(mesh):
    in_specs = (
        P("req", "head"),
        P("req", "head", None, None),
        P("req", None, "head"),
        P("req", None, "head"),
        P("req", "head"),
        P("req", "head"),
        P("req", "head"),
        P("req", "head"),
        P(None, "head"),
        P("head"),
        P(None, "head"),
        P("head"),
        P("head"),
        P("head"),
        P("head"),
        P("head"),
        P("head", "req"),
        P("req", None),
        P("req", None),
        P("req"),
        P("req"),
    )
    out_specs = (P("req", "head"), P("req", "head", None, None))
    return jax.shard_map(
        on_device, mesh=mesh, in_specs=in_specs, out_specs=out_specs, check_vma=False
    )
```

profile of v0, /device:TPU:16, one launch (start us, length us, event | category | flops | bytes accessed | tf_op | source)
XLA Modules:
  0.0 575.6 jit_solution(14914639633637729458)
XLA Ops:
  7.2 0.7 all-gather.6.cloned.1.call-update
  8.0 0.1 collective-permute-start.2
  8.1 1.7 collective-permute-done.2
  9.8 1.9 maximum_select_fusion
  11.9 0.7 all-gather.8.cloned.1.call-update
  12.6 0.5 all-gather.12.cloned.1.call-update
  13.2 0.5 all-gather.14.cloned.1.call-update
  13.8 0.2 collective-permute-start.1
  14.0 0.4 collective-permute-start.3
  14.4 0.1 collective-permute-start
  14.6 0.2 fusion.89
  14.9 0.6 iota_compare_fusion.9
  15.5 0.4 convolution_minimum_fusion.5
  15.9 0.2 convolution_minimum_fusion.4
  16.1 0.2 convolution_minimum_fusion.3
  16.3 0.2 convolution_minimum_fusion.2
  16.5 0.2 convolution_minimum_fusion.1
  16.7 0.2 fusion.95
  16.9 0.1 fusion.67
  17.2 0.6 fusion.93
  17.8 0.2 fusion.46
  18.1 0.2 fusion.45
  18.3 0.2 fusion.44
  18.6 23.6 %all_gather.20 = bf16[8192,16]{0,1:T(8,128)(2,1)S(1)} all-gather(bf16[512,16]{0,1:T(8,128)(2,1)S(1)} %copy-done.12), channel_id=1, replica_groups=mesh['req'=16,'head'=16] {'req'}, dimensions={0}, use_global_device_ids=true | all-gather | bytes 278528 | tf_op jit(solution)/shard_map/all_gather | solution.py:139
  42.2 0.7 copy.40
  43.0 9.3 %all-gather.6.cloned.1.call-done = bf16[128,8192]{1,0:T(8,128)(2,1)} async-done(((bf16[128,512]{1,0:T(8,128)(2,1)}), bf16[128,8192]{1,0:T(8,128)(2,1)}) %all-gather.6.cloned.1.call-update) | async-done | bytes 2097168 | tf_op jit(solution)/shard_map/all_gather | solution.py:112
  52.3 2.4 fusion.16
  54.9 0.2 fusion.54
  55.1 0.1 fusion.69
  55.2 0.1 select_multiply_fusion
  55.4 74.1 %all-gather.10.cloned.1.call-done = bf16[8192,512]{1,0:T(8,128)(2,1)} async-done(((bf16[512,512]{1,0:T(8,128)(2,1)}), bf16[8192,512]{1,0:T(8,128)(2,1)}) %all-gather.10.cloned.1.call-update) | async-done | bytes 8388624 | tf_op jit(solution)/shard_map/all_gather | solution.py:138
  129.5 4.8 convolution_convert_fusion.2
  134.3 0.3 fusion.100
  134.6 0.3 fusion.99
  134.8 0.3 fusion.101
  135.1 0.2 fusion.11
  135.4 0.2 fusion.10
  135.6 0.3 divide_multiply_fusion.1
  136.0 0.3 fusion.38
  136.2 2.8 convolution_multiply_fusion
  139.1 109.0 %all-gather.8.cloned.1.call-done = bf16[8192,1024]{1,0:T(8,128)(2,1)} async-done(((bf16[512,1024]{1,0:T(8,128)(2,1)}), bf16[8192,1024]{1,0:T(8,128)(2,1)}) %all-gather.8.cloned.1.call-update) | async-done | bytes 16777232 | tf_op jit(solution)/shard_map/all_gather | solution.py:137
  248.1 8.3 %convolution_convert_fusion.1 = bf16[128,1024]{1,0:T(8,128)(2,1)S(1)} fusion(bf16[128,8192]{1,0:T(8,128)(2,1)S(1)} %copy-done.2, bf16[8192,1024]{1,0:T(8,128)(2,1)} %all-gather.8.cloned.1.call-done), kind=kOutput, calls=%fused_computation.17 | convolution fusion | flops 2147614720 | bytes 19136512 | tf_op jit(solution)/shard_map/dot_general | solution.py:75
  256.4 0.3 fusion.96
  256.8 0.3 fusion.97
  257.1 0.3 fusion.98
  257.6 0.3 fusion.8
  257.9 0.3 fusion.7
  258.2 0.4 divide_multiply_fusion
  258.6 1.3 copy.59
  259.9 106.6 %all-gather.12.cloned.1.call-done = bf16[8192,1024]{1,0:T(8,128)(2,1)} async-done(((bf16[512,1024]{1,0:T(8,128)(2,1)}), bf16[8192,1024]{1,0:T(8,128)(2,1)}) %all-gather.12.cloned.1.call-update) | async-done | bytes 16777232 | tf_op jit(solution)/shard_map/all_gather | solution.py:136
  366.5 8.3 %fusion.9 = f32[128,1024]{1,0:T(8,128)S(1)} fusion(bf16[128,8192]{1,0:T(8,128)(2,1)S(1)} %copy-done.2, bf16[8192,1024]{1,0:T(8,128)(2,1)} %all-gather.12.cloned.1.call-done), kind=kOutput, calls=%fused_computation.16 | convolution fusion | flops 2147745792 | bytes 19398656 | tf_op jit(solution)/shard_map/dot_general | solution.py:75
  374.8 0.5 reshape.152
  375.3 1.4 copy.50
  376.7 4.8 multiply_reduce_fusion
  381.6 1.8 copy.48
  383.4 0.3 reshape.150
  383.8 109.2 %all-gather.14.cloned.1.call-done = bf16[1024,8192]{1,0:T(8,128)(2,1)} async-done(((bf16[1024,512]{1,0:T(8,128)(2,1)}), bf16[1024,8192]{1,0:T(8,128)(2,1)}) %all-gather.14.cloned.1.call-update) | async-done | bytes 16777232 | tf_op jit(solution)/shard_map/all_gather | solution.py:180
  493.1 10.3 %fusion.31 = f32[128,8192]{1,0:T(8,128)} fusion(bf16[1024,8192]{1,0:T(8,128)(2,1)} %all-gather.14.cloned.1.call-done, f32[128,1024]{1,0:T(8,128)S(1)} %reshape.150, f32[128,1024]{1,0:T(8,128)S(1)} %fusion.9, f32[1024]{0:T(1024)S(1)} %copy-done.7, f32[128]{0:T(128)S(1)} %mul.218), kind=kOutput, calls=%fused_computation.54 | convolution fusion | flops 2148532224 | bytes 22024704 | tf_op jit(solution)/shard_map/dot_general | solution.py:178
  503.3 0.6 copy-done.15
  504.0 0.9 copy-done.4
  504.9 0.3 copy-done.6
  505.2 3.3 multiply_add_fusion
  508.4 58.7 %reduce-scatter.2.cloned.1.call-done = f32[128,512]{1,0:T(8,128)} async-done(((f32[128,8192]{1,0:T(8,128)}), f32[128,512]{1,0:T(8,128)}) %reduce-scatter.2.cloned.1.call-update) | async-done | bytes 262160 | tf_op jit(solution)/shard_map/reduce_scatter | solution.py:183
  567.2 1.6 convert_element_type.106
  (104 shorter events, 0.9 us)
Async XLA Ops:
  7.2 250.3 %copy-start = (bf16[2,3,1024]{2,0,1:T(2,128)(2,1)S(1)}, bf16[2,3,1024]{2,0,1:T(2,128)(2,1)}, u32[]{:S(2)}) copy-start(bf16[2,3,1024]{2,0,1:T(2,128)(2,1)} %param.23) | copy-start | bytes 36868
  7.2 45.1 %all-gather.6.cloned.1.call-start = ((), (), s32[]{:S(2)}) async-start(), calls=%async_computation.1 | async-start | bytes 2228224 | tf_op jit(solution)/shard_map/all_gather | solution.py:112
  7.9 121.6 %all-gather.10.cloned.1.call-start = ((), (), s32[]{:S(2)}) async-start(), calls=%async_computation.3 | async-start | bytes 8912896 | tf_op jit(solution)/shard_map/all_gather | solution.py:138
  8.0 1.8 collective-permute-start.2
  11.7 2.1 copy-start.30
  11.7 2.3 copy-start.23
  11.7 2.7 copy-start.32
  11.7 2.8 copy-start.33
  11.8 2.8 copy-start.31
  11.8 3.1 copy-start.34
  11.8 3.7 copy-start.9
  11.8 5.3 copy-start.8
  11.8 236.2 %all-gather.8.cloned.1.call-start = ((), (), s32[]{:S(2)}) async-start(), calls=%async_computation.2 | async-start | bytes 17825792 | tf_op jit(solution)/shard_map/all_gather | solution.py:137
  12.6 6.0 %copy-start.12 = (bf16[512,16]{0,1:T(8,128)(2,1)S(1)}, bf16[512,16]{0,1:T(8,128)(2,1)}, u32[]{:S(2)}) copy-start(bf16[512,16]{0,1:T(8,128)(2,1)} %param.28) | copy-start | bytes 49156
  12.6 29.6 %copy-start.29 = (bf16[1024]{0:T(1024)(128)(2,1)S(1)}, bf16[1024]{0:T(1024)(128)(2,1)}, u32[]{:S(2)}) copy-start(bf16[1024]{0:T(1024)(128)(2,1)} %param.30) | copy-start | bytes 6148
  12.6 29.6 %copy-start.35 = (f32[16]{0:T(128)S(1)}, f32[16]{0:T(128)}, u32[]{:S(2)}) copy-start(f32[16]{0:T(128)} %param.34) | copy-start | bytes 196
  12.6 353.9 %all-gather.12.cloned.1.call-start = ((), (), s32[]{:S(2)}) async-start(), calls=%async_computation.4 | async-start | bytes 17825792 | tf_op jit(solution)/shard_map/all_gather | solution.py:136
  13.2 479.9 %all-gather.14.cloned.1.call-start = ((), (), s32[]{:S(2)}) async-start(), calls=%async_computation.5 | async-start | bytes 17825792 | tf_op jit(solution)/shard_map/all_gather | solution.py:180
  13.8 553.4 %reduce-scatter.2.cloned.1.call-start = ((), (), s32[]{:S(2)}) async-start(), calls=%async_computation.6 | async-start | bytes 4456448 | tf_op jit(solution)/shard_map/reduce_scatter | solution.py:183
  13.8 29.1 %collective-permute-start.1 = (bf16[4,256]{1,0:T(4,128)(2,1)S(1)}, bf16[4,256]{1,0:T(4,128)(2,1)S(1)}, u32[]{:S(2)}, u32[]{:S(2)}) collective-permute-start(bf16[4,256]{1,0:T(4,128)(2,1)S(1)} %copy-done.30), channel_id=1, source_target_pairs={{0,1},{1,0},{2,3},{3,2},{4,5},{5,4},{6,7},{7,6},{8,9},{9,8},{10,11... | collective-permute-start | bytes 6152 | tf_op jit(solution)/shard_map/ppermute | solution.py:31
  14.0 28.9 %collective-permute-start.3 = (bf16[2,3,256]{2,0,1:T(2,128)(2,1)S(1)}, bf16[2,3,256]{2,0,1:T(2,128)(2,1)S(1)}, u32[]{:S(2)}, u32[]{:S(2)}) collective-permute-start(bf16[2,3,256]{2,0,1:T(2,128)(2,1)S(1)} %copy-done.23), channel_id=1, source_target_pairs={{0,1},{1,0},{2,3},{3,2},{4,5},{5,4},{6,7},{7,6},{8,9},{9,8},{10,11... | collective-permute-start | bytes 9224 | tf_op jit(solution)/shard_map/ppermute | solution.py:31
  14.4 28.5 %collective-permute-start = (bf16[256]{0:T(256)(128)(2,1)S(1)}, bf16[256]{0:T(256)(128)(2,1)S(1)}, u32[]{:S(2)}, u32[]{:S(2)}) collective-permute-start(bf16[256]{0:T(256)(128)(2,1)S(1)} %copy-done.32), channel_id=1, source_target_pairs={{0,1},{1,0},{2,3},{3,2},{4,5},{5,4},{6,7},{7,6},{8,9},{9,8},{10,11... | collective-permute-start | bytes 1544 | tf_op jit(solution)/shard_map/ppermute | solution.py:31
  16.1 38.7 %copy-start.24 = (f32[16]{0:T(128)S(1)}, f32[16]{0:T(128)}, u32[]{:S(2)}) copy-start(f32[16]{0:T(128)} %param.33) | copy-start | bytes 196
  17.1 118.0 %copy-start.16 = (pred[2,64]{1,0:T(4,128)(4,1)}, pred[2,64]{1,0:T(4,128)(4,1)S(1)}, u32[]{:S(2)}) copy-start(pred[2,64]{1,0:T(4,128)(4,1)S(1)} %get-tuple-element.13) | copy-start | bytes 388
  17.1 118.2 %copy-start.25 = (pred[2,64]{1,0:T(4,128)(4,1)}, pred[2,64]{1,0:T(4,128)(4,1)S(1)}, u32[]{:S(2)}) copy-start(pred[2,64]{1,0:T(4,128)(4,1)S(1)} %get-tuple-element.14) | copy-start | bytes 388
  17.1 118.5 %copy-start.27 = (pred[2,64]{1,0:T(4,128)(4,1)}, pred[2,64]{1,0:T(4,128)(4,1)S(1)}, u32[]{:S(2)}) copy-start(pred[2,64]{1,0:T(4,128)(4,1)S(1)} %get-tuple-element.12) | copy-start | bytes 388
  17.2 118.2 %copy-start.18 = (f32[2,64]{1,0:T(2,128)}, f32[2,64]{1,0:T(2,128)S(1)}, u32[]{:S(2)}) copy-start(f32[2,64]{1,0:T(2,128)S(1)} %get-tuple-element.16) | copy-start | bytes 1540
  17.2 118.5 %copy-start.21 = (f32[2,64]{1,0:T(2,128)}, f32[2,64]{1,0:T(2,128)S(1)}, u32[]{:S(2)}) copy-start(f32[2,64]{1,0:T(2,128)S(1)} %get-tuple-element.15) | copy-start | bytes 1540
  52.3 77.2 %copy-start.2 = (bf16[128,8192]{1,0:T(8,128)(2,1)S(1)}, bf16[128,8192]{1,0:T(8,128)(2,1)}, u32[]{:S(2)}) copy-start(bf16[128,8192]{1,0:T(8,128)(2,1)} %all-gather.6.cloned.1.call-done) | copy-start | bytes 6291460
  55.2 79.0 %copy-start.14 = (f32[2,1,16]{2,1,0:T(1,128)}, f32[2,1,16]{2,1,0:T(1,128)S(1)}, u32[]{:S(2)}) copy-start(f32[2,1,16]{2,1,0:T(1,128)S(1)} %fusion.69) | copy-start | bytes 388
  134.5 1.7 copy-start.3
  256.4 1.2 copy-start.10
  256.4 1.2 copy-start.11
  256.4 1.2 copy-start.22
  256.4 1.2 copy-start.28
  256.4 1.5 copy-start.17
  257.1 1.0 copy-start.19
  257.1 1.0 copy-start.20
  257.1 1.0 copy-start.26
  374.7 2.0 copy-start.5
  374.8 2.0 copy-start.13
  374.8 2.0 copy-start.36
  374.8 1.9 copy-start.37
  381.6 111.5 %copy-start.7 = (f32[1024]{0:T(1024)S(1)}, f32[1024]{0:T(1024)}, u32[]{:S(2)}) copy-start(f32[1024]{0:T(1024)} %param.36) | copy-start | bytes 12292
  381.6 2.2 collective-permute-start.4
  503.3 0.7 copy-start.15
  503.3 1.6 copy-start.4
  503.3 1.9 copy-start.6
  504.0 64.8 %copy-start.1 = (bf16[2,3,1024]{2,0,1:T(2,128)(2,1)S(1)}, bf16[2,3,1024]{2,0,1:T(2,128)(2,1)}, u32[]{:S(2)}) copy-start(bf16[2,3,1024]{2,0,1:T(2,128)(2,1)} %param.23) | copy-start | bytes 36868
Sparse Core Ops, SparseCore 0:
  9.9 42.3 all-gather.5
  55.3 74.1 all-gather.9
  131.9 116.0 all-gather.7
  250.3 116.0 all-gather.11
  368.7 124.2 all-gather.13
  503.5 63.6 reduce-scatter.1
where the time goes:
time: 576 us
  waiting for transfers between devices  471 us (82%)
  matrix products  51.3 us (9%)
  blocking collectives  23.6 us (4%)
  between operations  14.9 us (3%)
  local copies, waits for them, and re-layouts  8.87 us (2%)
    all_gather x1, waiting for transfers between devices, on_device(): lax.all_gather(out_weight, 'req', axis=1, tiled=True)  109 us
    all_gather x1, waiting for transfers between devices, on_device(): lax.all_gather(weights[1], 'req', axis=0, tiled=True)  109 us
    all_gather x1, waiting for transfers between devices, on_device(): lax.all_gather(weights[0], 'req', axis=0, tiled=True)  107 us
    all_gather x1, waiting for transfers between devices, on_device(): lax.all_gather(weights[2], 'req', axis=0, tiled=True)  74.1 us
    reduce_scatter x1, waiting for transfers between devices, on_device(): lax.psum_scatter(terms, 'head', scatter_dimension=1, tiled=True)  58.7 us
    dot_general x4, matrix products, add_rows(): jnp.dot(gathered, piece, preferred_element_type=jnp.float32)  23.7 us
    all_gather x1, blocking collectives, on_device(): lax.all_gather(weights[3], 'req', axis=0, tiled=True)  23.6 us
  transfers between devices with their start and end apart: 11, of which 7 were waited for; matrix products, arithmetic and copies ran while one was open for 9% of the time, Pallas kernels for 0%

commit v1 on v0

--- a/solution.py
+++ b/solution.py
@@ -1,6 +1,10 @@
+import functools
+
 import jax
 import jax.numpy as jnp
 from jax import lax
+from jax.experimental import pallas as pl
+from jax.experimental.pallas import tpu as pltpu
 from jax.sharding import PartitionSpec as P
 
 HEAD_DIM = 64
@@ -8,17 +12,456 @@
 GROUPS = 8
 CONV = 4
 INNER = 16384
-
-
+MESH = pl.DeviceIdType.MESH
+F32 = jnp.float32
+BF16 = jnp.bfloat16
 HIGHEST_PRECISION = lax.Precision.HIGHEST
-
-
-def shortened(shard):
-
-    def short(part):
-        return part.astype(jnp.bfloat16) if part.dtype == jnp.float32 else part
-
-    return jax.tree.map(short, shard)
+UNITS = (
+    ("group", 0, 128, 128),
+    ("inner", 0, 512, 256),
+    ("inner", 256, 768, 256),
+    ("gate", 0, 512, 256),
+    ("gate", 256, 768, 256),
+)
+
+
+class Place:
+    def __init__(self):
+        self.r = lax.axis_index("req")
+        self.h = lax.axis_index("head")
+        self.y, self.x = self.r // 4, self.r % 4
+        self.z, self.c = self.h // 2, self.h % 2
+
+    def at(self, dy=0, dx=0, dz=0, dc=0):
+        y, x = (self.y + dy) % 4, (self.x + dx) % 4
+        z, c = (self.z + dz) % 8, (self.c + dc) % 2
+        return (y * 4 + x, z * 2 + c)
+
+
+def remote(src, dst, send, recv, device):
+    return pltpu.make_async_remote_copy(
+        src_ref=src, dst_ref=dst, send_sem=send, recv_sem=recv,
+        device_id=device, device_id_type=MESH,
+    )
+
+
+def meet(devices, maybe=()):
+    barrier = pltpu.get_barrier_semaphore()
+    for device in devices:
+        pl.semaphore_signal(barrier, inc=1, device_id=device, device_id_type=MESH)
+    for device, here in maybe:
+        @pl.when(here)
+        def _():
+            pl.semaphore_signal(barrier, inc=1, device_id=device, device_id_type=MESH)
+    pl.semaphore_wait(barrier, len(devices) + sum(jnp.where(here, 1, 0) for _, here in maybe))
+
+
+def dot(a, b):
+    return jnp.dot(a, b, preferred_element_type=F32)
+
+
+class Unit:
+    def __init__(self, place, first, weight, column, width, tokens, out, bufs, send, recv):
+        self.p, self.first = place, first
+        self.a, self.b = (place.x, place.y) if first == "x" else (place.y, place.x)
+        self.weight, self.column, self.width = weight, column, width
+        self.tokens, self.out = tokens, out
+        (self.s1, self.rf, self.s2p, self.s2m, self.rgp, self.rgm, self.q,
+         self.s3, self.rh, self.s4p, self.s4m, self.rip, self.rim) = bufs
+        self.send, self.recv = send, recv
+        self.copies = {}
+
+    def along(self, which, step):
+        name = self.first if which == "a" else ("y" if self.first == "x" else "x")
+        return self.p.at(dy=step) if name == "y" else self.p.at(dx=step)
+
+    def part(self, dest_a, b):
+        slot = 4 * b + dest_a if self.first == "x" else 4 * dest_a + b
+        return dot(
+            self.tokens[slot], self.weight[:, self.column : self.column + self.width]
+        )
+
+    def put(self, k, src, dst, which, step):
+        copy = remote(src, dst, self.send.at[k], self.recv.at[k], self.along(which, step))
+        copy.start()
+        self.copies[k] = copy
+
+    def stage1(self):
+        far = (self.a + 2) % 4
+
+        @pl.loop(0, 4)
+        def _(b):
+            self.s1[b] = self.part(far, b).astype(BF16)
+
+        self.put(0, self.s1.at[0:2], self.rf.at[0:2], "a", 1)
+        self.put(1, self.s1.at[2:4], self.rf.at[2:4], "a", -1)
+
+    def stage2(self):
+        self.copies[0].wait_recv()
+        self.copies[1].wait_recv()
+        up, down = (self.a + 1) % 4, (self.a + 3) % 4
+
+        @pl.loop(0, 2)
+        def _(b):
+            self.s2p[b] = (self.part(up, b) + self.rf[b].astype(F32)).astype(BF16)
+            self.s2p[b + 2] = self.part(up, b + 2).astype(BF16)
+            self.s2m[b] = self.part(down, b).astype(BF16)
+            self.s2m[b + 2] = (self.part(down, b + 2) + self.rf[b + 2].astype(F32)).astype(BF16)
+
+        self.put(2, self.s2p, self.rgp, "a", 1)
+        self.put(3, self.s2m, self.rgm, "a", -1)
+
+    def stage3(self):
+        self.copies[2].wait_recv()
+        self.copies[3].wait_recv()
+
+        @pl.loop(0, 4)
+        def _(b):
+            self.q[b] = self.part(self.a, b) + self.rgp[b].astype(F32) + self.rgm[b].astype(F32)
+
+        self.s3[...] = self.q[(self.b + 2) % 4].astype(BF16)
+        self.put(4, self.s3.at[0:64], self.rh.at[0:64], "b", 1)
+        self.put(5, self.s3.at[64:128], self.rh.at[64:128], "b", -1)
+
+    def stage4(self):
+        self.copies[4].wait_recv()
+        self.copies[5].wait_recv()
+        up, down = (self.b + 1) % 4, (self.b + 3) % 4
+        self.s4p[0:64] = (self.q[up, 0:64] + self.rh[0:64].astype(F32)).astype(BF16)
+        self.s4p[64:128] = self.q[up, 64:128].astype(BF16)
+        self.s4m[0:64] = self.q[down, 0:64].astype(BF16)
+        self.s4m[64:128] = (self.q[down, 64:128] + self.rh[64:128].astype(F32)).astype(BF16)
+        self.put(6, self.s4p, self.rip, "b", 1)
+        self.put(7, self.s4m, self.rim, "b", -1)
+
+    def stage5(self):
+        self.copies[6].wait_recv()
+        self.copies[7].wait_recv()
+        total = self.q[self.b] + self.rip[...].astype(F32) + self.rim[...].astype(F32)
+        self.out[:, self.column : self.column + self.width] = total.astype(BF16)
+
+    def finish(self):
+        for copy in self.copies.values():
+            copy.wait_send()
+
+
+def unit_scratch(width):
+    def block(n, dtype=BF16):
+        return pltpu.VMEM((n, 128, width), dtype)
+
+    flat = pltpu.VMEM((128, width), BF16)
+    return [block(4)] * 6 + [block(4, F32)] + [flat] * 6
+
+
+def input_kernel(*refs):
+    (tok, wgate, winner, wgroup, wstep, wout,
+     gate, inner, group, step, wx, wy,
+     tg, st, sr,
+     tsem_s, tsem_r, zs, zr, cs, cr, ss, sr_sem, os, orr, gs, gr, us, ur, local) = refs[:30]
+    bufs = refs[30:]
+    p = Place()
+    r, h, z, c = p.r, p.h, p.z, p.c
+    other = (h // 4) * 4 + h % 4
+    moved = r != h
+    req_peers = [((r + j) % 16, h) for j in range(1, 16)]
+    meet(
+        req_peers + [p.at(dz=1), p.at(dz=-1), p.at(dc=1)],
+        [((other, r), moved)],
+    )
+    turn = remote(tok, tg.at[r], tsem_s, tsem_r, (other, r))
+
+    @pl.when(moved)
+    def _():
+        turn.start()
+
+    @pl.when(jnp.logical_not(moved))
+    def _():
+        pltpu.make_async_copy(tok, tg.at[r], local).start()
+
+    outs = []
+    for ax, full, lo in (("x", wx, 0), ("y", wy, 256)):
+        me = p.x if ax == "x" else p.y
+        half = wout.at[:, lo : lo + 256]
+        for i, d in enumerate((1, -1)):
+            peer = p.at(dx=d) if ax == "x" else p.at(dy=d)
+            k = len(outs)
+            copy = remote(half, full.at[me], os.at[k], orr.at[k], peer)
+            copy.start()
+            outs.append(copy)
+        keep = pltpu.make_async_copy(half, full.at[me], os.at[len(outs) + 6])
+        keep.start()
+        outs.append(keep)
+
+    @pl.when(moved)
+    def _():
+        turn.wait()
+
+    @pl.when(jnp.logical_not(moved))
+    def _():
+        pltpu.make_async_copy(tok, tg.at[r], local).wait()
+
+    def block(dz):
+        return 2 * ((z + dz) % 8) + c
+
+    cores = []
+
+    def to_core(dz):
+        k = len(cores)
+        copy = remote(tg.at[block(dz)], tg.at[block(dz)], cs.at[k], cr.at[k], p.at(dc=1))
+        copy.start()
+        cores.append(copy)
+
+    ring = []
+
+    def hop(dz, d, lo, n):
+        k = len(ring)
+        ref = tg.at[block(dz), lo : lo + n]
+        copy = remote(ref, ref, zs.at[k], zr.at[k], p.at(dz=d))
+        copy.start()
+        ring.append(copy)
+        return copy
+
+    plus, minus = hop(0, 1, 0, 128), hop(0, -1, 0, 128)
+    to_core(0)
+    for s in range(1, 4):
+        rows = 128 if s < 3 else 64
+        plus.wait_recv()
+        plus = hop(-s, 1, 0, rows)
+        minus.wait_recv()
+        minus = hop(s, -1, 128 - rows, rows)
+        to_core(-s)
+        to_core(s)
+    plus.wait_recv()
+    minus.wait_recv()
+    to_core(4)
+    for k, (ax, full, d, lo) in enumerate(
+        (("x", wx, 1, 0), ("x", wx, -1, 512), ("y", wy, 1, 0), ("y", wy, -1, 512))
+    ):
+        first = outs[(0, 1, 3, 4)[k]]
+        first.wait_recv()
+        me = p.x if ax == "x" else p.y
+        peer = p.at(dx=d) if ax == "x" else p.at(dy=d)
+        ref = full.at[(me - d) % 4, lo : lo + 512]
+        copy = remote(ref, ref, gs.at[k], gr.at[k], peer)
+        copy.start()
+        outs.append(copy)
+    for copy in cores:
+        copy.wait_recv()
+
+    @pl.loop(0, 16)
+    def _(k):
+        st[k] = lax.dot_general(
+            wstep[...], tg[k], (((1,), (1,)), ((), ())), preferred_element_type=F32
+        )
+
+    @pl.loop(1, 16)
+    def _(j):
+        to = (r + j) % 16
+        remote(st.at[to], sr.at[j], ss, sr_sem, (to, h)).start()
+
+    sources = {"group": wgroup, "inner": winner, "gate": wgate}
+    results = {"group": group, "inner": inner, "gate": gate}
+    units = []
+    for i, (name, xcol, ycol, width) in enumerate(UNITS):
+        pair = []
+        for j, (first, col) in enumerate((("x", xcol), ("y", ycol))):
+            n = 2 * i + j
+            out = group.at[p.c] if name == "group" else results[name]
+            pair.append(Unit(p, first, sources[name], col, width, tg, out,
+                             bufs[13 * n : 13 * n + 13], us.at[n], ur.at[n]))
+        units.append(pair)
+    count = len(units)
+    swap = remote(group.at[p.c], group.at[p.c], tsem_s, tsem_r, p.at(dc=1))
+    for t in range(-1, count + 3):
+        for stage, lag in ((1, -1), (2, 0), (3, 1), (4, 2), (5, 3)):
+            if 0 <= t - lag < count:
+                for unit in units[t - lag]:
+                    getattr(unit, "stage%d" % stage)()
+                if stage == 5 and t - lag == 0:
+                    swap.start()
+    for pair in units:
+        for unit in pair:
+            unit.finish()
+    swap.wait()
+    tail = sr.at[1:16]
+    pltpu.make_async_copy(tail, tail, sr_sem).wait()
+    sums = st[r]
+    for j in range(1, 16):
+        sums = sums + sr[j]
+    step[...] = sums
+    pltpu.make_async_copy(tail, tail, ss).wait()
+    for k, copy in enumerate(outs):
+        if k in (2, 5):
+            copy.wait()
+        else:
+            copy.wait_send()
+            if k > 5:
+                copy.wait_recv()
+    for copy in cores + ring:
+        copy.wait_send()
+
+
+def project(tokens, wgate, winner, wgroup, wstep_t, wout):
+    vmem = pl.BlockSpec(memory_space=pltpu.VMEM)
+    hbm = pl.BlockSpec(memory_space=pl.ANY)
+    dma = pltpu.SemaphoreType.DMA
+    scratch = [
+        pltpu.VMEM((16, 128, 512), BF16),
+        pltpu.VMEM((16, 16, 128), F32),
+        pltpu.VMEM((16, 16, 128), F32),
+        dma, dma, dma((8,)), dma((8,)), dma((8,)), dma((8,)), dma, dma,
+        dma((12,)), dma((6,)), dma((4,)), dma((4,)),
+        dma((2 * len(UNITS), 8)), dma((2 * len(UNITS), 8)), dma,
+    ]
+    for _, _, _, width in UNITS:
+        scratch += unit_scratch(width) * 2
+    shape = jax.ShapeDtypeStruct
+    return pl.pallas_call(
+        input_kernel,
+        name="input_projections",
+        out_shape=(
+            shape((128, 1024), BF16), shape((128, 1024), BF16), shape((2, 128, 256), BF16),
+            shape((16, 128), F32), shape((4, 1024, 256), BF16), shape((4, 1024, 256), BF16),
+        ),
+        in_specs=[vmem] * 5 + [hbm],
+        out_specs=(vmem,) * 4 + (hbm,) * 2,
+        scratch_shapes=scratch,
+        compiler_params=pltpu.CompilerParams(
+            collective_id=0, has_side_effects=True, vmem_limit_bytes=56 * 2**20
+        ),
+    )(tokens, wgate, winner, wgroup, wstep_t, wout)
+
+
+def output_kernel(norm, wx, wy, out,
+                  nx, ny, own, sent, got, zsend_p, zsend_m, zgot_p, zgot_m, fin, land,
+                  ns, nr, cs, cr, zs, zr, fs, fr, local):
+    p = Place()
+    r, h, y, x, z, c = p.r, p.h, p.y, p.x, p.z, p.c
+    hy, hx = h // 4, h % 4
+    goal = ((hy * 4 + x, y * 4 + hx), (y * 4 + hx, hy * 4 + x))
+    away = (hy != y, hx != x)
+    meet(
+        [p.at(dy=d) for d in (1, 2, 3)] + [p.at(dx=d) for d in (1, 2, 3)]
+        + [p.at(dz=1), p.at(dz=-1), p.at(dc=1)],
+        [(goal[0], away[0]), (goal[1], away[1])],
+    )
+    copies = []
+    for d in (1, 3, 2):
+        for full, peer in ((ny.at[y], p.at(dy=d)), (nx.at[x], p.at(dx=d))):
+            k = len(copies)
+            copy = remote(norm, full, ns.at[k], nr.at[k], peer)
+            copy.start()
+            copies.append(copy)
+    nx[x] = norm[...]
+    ny[y] = norm[...]
+
+    def shard(zz, cc):
+        s = 2 * zz + cc
+        i, j = s // 4, s % 4
+        return dot(ny[i], wx[j]), dot(nx[j], wy[i])
+
+    for copy in copies:
+        copy.wait_recv()
+
+    @pl.loop(0, 8)
+    def _(zz):
+        left, right = shard(zz, 1 - c)
+        sent[zz, 0] = left.astype(BF16)
+        sent[zz, 1] = right.astype(BF16)
+
+    swap = remote(sent, got, cs, cr, p.at(dc=1))
+    swap.start()
+
+    @pl.loop(0, 8)
+    def _(zz):
+        left, right = shard(zz, c)
+        own[zz, 0] = left
+        own[zz, 1] = right
+
+    swap.wait_recv()
+
+    def mine(dz, half):
+        zz = (z + dz) % 8
+        return own[zz, half] + got[zz, half].astype(F32)
+
+    ring = []
+
+    def hop(src, dst, d):
+        k = len(ring)
+        copy = remote(src, dst, zs.at[k], zr.at[k], p.at(dz=d))
+        copy.start()
+        ring.append(copy)
+        return copy
+
+    zsend_p[0, 0] = mine(4, 0).astype(BF16)
+    plus = hop(zsend_p.at[0, 0], zgot_p.at[0, 0], 1)
+    zsend_m[0, 1] = mine(4, 1).astype(BF16)
+    minus = hop(zsend_m.at[0, 1], zgot_m.at[0, 1], -1)
+    for s in (1, 2, 3):
+        plus.wait_recv()
+        zsend_p[s, 0] = (mine(4 - s, 0) + zgot_p[s - 1, 0].astype(F32)).astype(BF16)
+        if s == 1:
+            zsend_p[s, 1] = mine(4 - s, 1).astype(BF16)
+        else:
+            zsend_p[s, 1] = (mine(4 - s, 1) + zgot_p[s - 1, 1].astype(F32)).astype(BF16)
+        plus = hop(zsend_p.at[s], zgot_p.at[s], 1)
+        minus.wait_recv()
+        if s == 1:
+            zsend_m[s, 0] = mine(s - 4, 0).astype(BF16)
+        else:
+            zsend_m[s, 0] = (mine(s - 4, 0) + zgot_m[s - 1, 0].astype(F32)).astype(BF16)
+        zsend_m[s, 1] = (mine(s - 4, 1) + zgot_m[s - 1, 1].astype(F32)).astype(BF16)
+        minus = hop(zsend_m.at[s], zgot_m.at[s], -1)
+    plus.wait_recv()
+    minus.wait_recv()
+    for half in (0, 1):
+        fin[half] = (
+            mine(0, half) + zgot_p[3, half].astype(F32) + zgot_m[3, half].astype(F32)
+        ).astype(BF16)
+        move = remote(fin.at[half], land.at[half], fs.at[half], fr.at[half], goal[half])
+
+        @pl.when(away[half])
+        def _():
+            move.start()
+
+        @pl.when(jnp.logical_not(away[half]))
+        def _():
+            land[half] = fin[half]
+
+    for half in (0, 1):
+        move = remote(fin.at[half], land.at[half], fs.at[half], fr.at[half], goal[half])
+
+        @pl.when(away[half])
+        def _():
+            move.wait()
+
+        out[:, 256 * half : 256 * half + 256] = land[half]
+    for copy in copies + ring + [swap]:
+        copy.wait_send()
+
+
+def finish(normed, wx, wy):
+    vmem = pl.BlockSpec(memory_space=pltpu.VMEM)
+    dma = pltpu.SemaphoreType.DMA
+    return pl.pallas_call(
+        output_kernel,
+        name="output_projection",
+        out_shape=jax.ShapeDtypeStruct((128, 512), BF16),
+        in_specs=[vmem] * 3,
+        out_specs=vmem,
+        scratch_shapes=[
+            pltpu.VMEM((4, 128, 1024), BF16), pltpu.VMEM((4, 128, 1024), BF16),
+            pltpu.VMEM((8, 2, 128, 256), F32),
+            pltpu.VMEM((8, 2, 128, 256), BF16), pltpu.VMEM((8, 2, 128, 256), BF16),
+            pltpu.VMEM((4, 2, 128, 256), BF16), pltpu.VMEM((4, 2, 128, 256), BF16),
+            pltpu.VMEM((4, 2, 128, 256), BF16), pltpu.VMEM((4, 2, 128, 256), BF16),
+            pltpu.VMEM((2, 128, 256), BF16), pltpu.VMEM((2, 128, 256), BF16),
+            dma((6,)), dma((6,)), dma, dma, dma((8,)), dma((8,)), dma((2,)), dma((2,)), dma,
+        ],
+        compiler_params=pltpu.CompilerParams(
+            collective_id=1, has_side_effects=True, vmem_limit_bytes=48 * 2**20
+        ),
+    )(normed, wx, wy)
 
 
 def from_partner(block, axis, stride):
@@ -68,16 +511,6 @@
     return jax.nn.silu(summed)
 
 
-def make_adder(gathered):
-
-    def add_rows(totals, pieces, start):
-        return tuple(
-            (jnp.dot(gathered, piece, preferred_element_type=jnp.float32) for piece in pieces)
-        )
-
-    return add_rows
-
-
 def join_halves(mine, partner, upper_half):
     return jnp.where(
         upper_half == 1,
@@ -87,64 +520,31 @@
 
 
 def on_device(
-    tokens,
-    prior_state,
-    conv_inner_state,
-    conv_group_state,
-    gate_weight,
-    inner_weight,
-    group_weight,
-    step_weight,
-    conv_inner_weight,
-    conv_inner_bias,
-    conv_group_weight,
-    conv_group_bias,
-    step_bias,
-    decay_rate,
-    skip_gain,
-    norm_gain,
-    out_weight,
-    parents,
-    accepted_path,
-    path_length,
-    tree_size,
+    tokens, prior_state, conv_inner_state, conv_group_state, gate_weight, inner_weight,
+    group_weight, step_weight, conv_inner_weight, conv_inner_bias, conv_group_weight,
+    conv_group_bias, step_bias, decay_rate, skip_gain, norm_gain, out_weight, parents,
+    accepted_path, path_length, tree_size,
 ):
-    gathered = lax.all_gather(tokens, "head", axis=1, tiled=True)
     request_count, node_count = parents.shape
-    token_rows = gathered.shape[0]
+    token_rows = tokens.shape[0]
     position = lax.axis_index("head")
-    add_rows = make_adder(gathered)
     parent_map, reach, node_depth = tree_maps(parents)
-    group_parts = (group_weight, conv_group_weight, conv_group_bias, conv_group_state)
-    bit_number = 0
-    partner = jax.tree.map(
-        lambda part, own: part.astype(own.dtype),
-        from_partner(shortened(group_parts), "head", bit_number),
-        group_parts,
-    )
-    upper_half = position >> bit_number & 1
-    group_parts = tuple(
-        (
-            join_halves(mine, other_part, upper_half)
-            for mine, other_part in zip(group_parts, partner)
-        )
-    )
-    weights = (gate_weight, inner_weight, group_parts[0], step_weight)
-    sums = add_rows(
-        tuple((jnp.zeros((token_rows, weight.shape[1]), jnp.float32) for weight in weights)),
-        (
-            lax.all_gather(weights[0], "req", axis=0, tiled=True),
-            lax.all_gather(weights[1], "req", axis=0, tiled=True),
-            lax.all_gather(weights[2], "req", axis=0, tiled=True),
-            lax.all_gather(weights[3], "req", axis=0, tiled=True),
-        ),
-        jnp.int32(0),
-    )
-    gate_raw, inner_raw, group_raw, step_raw = (
-        summed.astype(jnp.bfloat16).reshape(request_count, node_count, -1) for summed in sums
-    )
+    group_parts = (conv_group_weight, conv_group_bias, conv_group_state)
+    partner = jax.tree.map(lambda part: from_partner(part, "head", 0), group_parts)
+    upper_half = position & 1
+    group_taps, group_bias, group_state = (
+        join_halves(mine, other_part, upper_half)
+        for mine, other_part in zip(group_parts, partner)
+    )
+    gate_raw, inner_raw, group_raw, step_raw, wx, wy = project(
+        tokens, gate_weight, inner_weight, group_weight, step_weight.T, out_weight
+    )
+    shaped = (request_count, node_count, -1)
+    gate_raw, inner_raw = gate_raw.reshape(shaped), inner_raw.reshape(shaped)
+    group_raw = jnp.concatenate((group_raw[0], group_raw[1]), axis=-1).reshape(shaped)
+    step_raw = step_raw.astype(BF16).T.reshape(shaped)
     group_values = tree_conv(
-        group_raw, group_parts[3], parent_map, node_depth, group_parts[1], group_parts[2]
+        group_raw, group_state, parent_map, node_depth, group_taps, group_bias
     )
     channels = tree_conv(
         inner_raw, conv_inner_state, parent_map, node_depth, conv_inner_weight, conv_inner_bias
@@ -170,17 +570,10 @@
     output = jnp.where(valid[:, :, None, None], output, 0.0).reshape(request_count, node_count, -1)
     gated = output * jax.nn.silu(gate_raw.astype(jnp.float32))
     squares = jnp.sum(gated * gated, axis=-1)
-    bit_number = 0
-    squares = squares + from_partner(squares, "head", bit_number)
+    squares = squares + from_partner(squares, "head", 0)
     mean_square = squares / (INNER // GROUPS)
     normed = (gated * lax.rsqrt(mean_square + 1e-05)[..., None] * norm_gain).astype(jnp.bfloat16)
-    normed_flat = normed.reshape(token_rows, -1)
-    terms = jnp.dot(
-        normed_flat,
-        lax.all_gather(out_weight, "req", axis=1, tiled=True),
-        preferred_element_type=jnp.float32,
-    )
-    mixed = lax.psum_scatter(terms, "head", scatter_dimension=1, tiled=True).astype(jnp.bfloat16)
+    mixed = finish(normed.reshape(token_rows, -1), wx, wy)
     last_pick = slot_ids[None, :] == (path_length - 1)[:, None]
     leaf_node = jnp.sum(jnp.where(last_pick, accepted_path, 0), axis=1)
     leaf_row = (slot_ids[None, :] == leaf_node[:, None]).astype(jnp.float32)

time: 576 us -> 199 us (0.35)
  waiting for transfers between devices: 471 us -> 0.01 us
  Pallas kernels: 0 us -> 154 us
  matrix products: 51.3 us -> 24.8 us
  blocking collectives: 23.6 us -> 0 us
  between operations: 14.9 us -> 1.33 us
    all_gather x5 -> x0, waiting for transfers between devices: 408 us -> none  [the longest x1 109 us: on_device(): lax.all_gather(out_weight, 'req', axis=1, tiled=True)]
    pallas_call x0 -> x2, Pallas kernels: none -> 154 us  [the longest x1 107 us: project(): pl.pallas_call(input_kernel, name='input_projections', out_shape=(shape((...]
    reduce_scatter x1 -> x0, waiting for transfers between devices: 58.7 us -> none  [on_device(): lax.psum_scatter(terms, 'head', scatter_dimension=1, tiled=True)]
    dot_general x5 -> x0, matrix products: 34 us -> none  [the longest x4 23.7 us: add_rows(): jnp.dot(gathered, piece, preferred_element_type=jnp.float32)]
    all_gather x1 -> x0, blocking collectives: 23.6 us -> none  [on_device(): lax.all_gather(weights[3], 'req', axis=0, tiled=True)]
  transfers between devices with their start and end apart: 11 -> 4, of which waited for: 7 -> 0; matrix products, arithmetic and copies ran while one was open for 9% -> 14% of each run, Pallas kernels for 0% -> 54%
where the time goes in v1:
time: 199 us; the launch traced here: 198 us
  Pallas kernels  154 us (77%)
  matrix products  24.8 us (12%)
  local copies, waits for them, and re-layouts  10.8 us (5%)
  other arithmetic  5.84 us (3%)
    pallas_call x1, Pallas kernels, project(): pl.pallas_call(input_kernel, name='input_projections', out_shape=(shape((...  107 us
    pallas_call x1, Pallas kernels, finish(): pl.pallas_call(output_kernel, name='output_projection', out_shape=jax.Sha...  47.2 us
    dot_general x6, matrix products, tree_conv(): jnp.einsum('rij,rjc->ric', ancestor_step, values, precision=HIGHEST_PRECI...  6.22 us
    dot_general x6, matrix products, tree_conv(): jnp.einsum('ris,rsc->ric', earlier.astype(jnp.float32), prior_inputs, pre...  5.1 us
  transfers between devices with their start and end apart: 4, of which 0 were waited for; matrix products, arithmetic and copies ran while one was open for 14% of the time, Pallas kernels for 54%

profile of v1, /device:TPU:16, one launch (start us, length us, event | category | flops | bytes accessed | tf_op | source)
XLA Modules:
  0.0 197.8 jit_solution(9126455619646839111)
XLA Ops:
  0.6 0.0 copy-start
  0.6 0.1 collective-permute-start.1
  0.7 0.5 collective-permute-start.2
  1.2 0.1 collective-permute-start
  1.4 0.9 fusion.40
  2.3 1.1 convolution_minimum_fusion.5
  3.4 0.2 convolution_minimum_fusion.4
  3.6 0.2 convolution_minimum_fusion.3
  3.8 0.2 convolution_minimum_fusion.2
  4.0 0.2 convolution_minimum_fusion.1
  4.2 0.2 fusion.92
  4.5 0.9 fusion.39
  5.4 0.0 copy-start.16
  5.4 107.1 %input_projections.1 = (bf16[128,1024]{1,0:T(8,128)(2,1)}, bf16[128,1024]{1,0:T(8,128)(2,1)}, bf16[2,128,256]{2,1,0:T(8,128)(2,1)}, f32[16,128]{1,0:T(8,128)}, b...) custom-call(bf16[128,512]{1,0:T(8,128)(2,1)} %refs_0_.1, bf16[512,1024]{1,0:T(8,128)(2,1)} %refs_1_.1, ...), custom_call_target="tpu_custom_call" | custom-call | tf_op jit(solution)/shard_map/input_projections/pallas_call | solution.py:319
  112.6 0.0 copy-start.15
  112.6 0.0 copy-start.27
  112.6 0.0 copy-start.29
  112.6 0.0 copy-start.30
  112.6 0.0 copy-start.24
  112.7 1.4 fusion.93
  114.0 0.0 copy-start.31
  114.1 1.4 fusion.94
  115.4 0.2 fusion.38
  115.7 1.3 fusion.95
  117.0 1.0 fusion.86
  118.0 0.3 fusion.87
  118.3 1.0 fusion.88
  119.3 0.1 reshape.152
  119.4 0.2 fusion.83
  119.6 0.1 compare_bitcast_fusion
  119.7 0.6 broadcast_compare_fusion
  120.3 0.1 fusion.61
  120.4 0.1 compare_select_fusion
  120.6 0.2 fusion.48
  120.8 0.1 fusion.63
  120.9 0.6 exp.42
  121.5 0.7 select_multiply_fusion
  122.2 0.6 iota_compare_fusion.9
  122.8 0.3 fusion.8
  123.1 0.3 fusion.7
  123.5 1.2 divide_multiply_fusion
  124.6 0.3 reshape.153
  124.9 1.4 copy.37
  126.4 1.5 copy.46
  127.9 1.4 copy.27
  129.3 0.7 fusion.84
  130.1 0.8 fusion.57
  130.8 0.8 broadcast_select_fusion
  131.6 1.2 fusion.9
  132.8 0.9 fusion.10
  133.7 1.3 divide_multiply_fusion.1
  135.0 0.0 copy-start.5
  135.1 0.3 fusion.32
  135.3 1.9 convolution_multiply_fusion
  137.3 0.0 copy-start.11
  137.3 3.4 %multiply_reduce_fusion = (f32[2,64]{1,0:T(2,128)S(1)}, f32[2,64,16,64]{1,3,2,0:T(8,128)}) fusion(f32[2,64,16,64]{1,3,2,0:T(8,128)S(1)} %copy-done.5, f32[2,64,16,64]{1,3,2,0:T(8,128)S(1)} %bitcast.73, f32[16]{0:T(128)S(1)} %copy-done.32, f32[2,64,16,64]{1,3,2,0:T(8,128)S(1)} %convolution_multiply_fusion, f32[2,64,16]{1,2,0:T(8,128)S(1)} %copy-done.14, ...), kind=kOutput, calls=%fused_computation.31 | convolution fusion | flops 102760320 | bytes 2155200 | tf_op jit(solution)/shard_map/rijh,rjhp->rihp/dot_general | solution.py:563
  140.7 3.3 %multiply_add_fusion = f32[2,16,64,256]{3,2,1,0:T(8,128)} fusion(f32[2,16,64,256]{3,2,1,0:T(8,128)S(1)} %copy-done.3, f32[2,64,16,64]{1,3,2,0:T(8,128)S(1)} %bitcast.74, f32[2,16]{1,0:T(2,128)S(1)} %copy-done.22, f32[2,64,16]{1,2,0:T(8,128)S(1)} %copy-done.11, f32[2,64,512]{2,1,0:T(8,128)S(1)} %divide_multiply_fusion.1), kind=kOutput, calls=%fused_computation | convolution fusion | flops 403832832 | bytes 5391360 | tf_op jit(solution)/shard_map/rjh,rjhp,rjn->rhpn/dot_general | solution.py:587
  144.0 1.9 copy.35
  145.8 1.1 reshape.151
  147.0 0.1 mul.218
  147.1 1.2 multiply_convert_fusion.norm
  148.3 1.6 copy-done.2
  149.9 47.2 %output_projection.1 = bf16[128,512]{1,0:T(8,128)(2,1)S(1)} custom-call(bf16[128,1024]{1,0:T(8,128)(2,1)S(1)} %multiply_convert_fusion.norm, bf16[4,1024,256]{2,1,0:T(8,128)(2,1)S(1)} %copy-done.1, bf16[4,1024,256]{2,1,0:T(8,128)(2,1)S(1)} %copy-done.2), custom_call_target="tpu_custom_call" | custom-call | tf_op jit(solution)/shard_map/output_projection/pallas_call | solution.py:446
  197.2 0.7 copy.69
  (74 shorter events, 0.2 us)
Async XLA Ops:
  0.6 122.2 %copy-start = (bf16[2,3,1024]{2,0,1:T(2,128)(2,1)S(1)}, bf16[2,3,1024]{2,0,1:T(2,128)(2,1)}, u32[]{:S(2)}) copy-start(bf16[2,3,1024]{2,0,1:T(2,128)(2,1)} %param.23) | copy-start | bytes 36868
  0.6 129.4 %collective-permute-start.1 = (bf16[4,256]{1,0:T(4,128)(2,1)}, bf16[4,256]{1,0:T(4,128)(2,1)}, u32[]{:S(2)}, u32[]{:S(2)}) collective-permute-start(bf16[4,256]{1,0:T(4,128)(2,1)} %param.31), channel_id=1, source_target_pairs={{0,1},{1,0},{2,3},{3,2},{4,5},{5,4},{6,7},{7,6},{8,9},{9,8},{10,11... | collective-permute-start | bytes 6152 | tf_op jit(solution)/shard_map/ppermute | solution.py:474
  0.7 130.1 %collective-permute-start.2 = (bf16[2,3,256]{2,0,1:T(2,128)(2,1)}, bf16[2,3,256]{2,0,1:T(2,128)(2,1)}, u32[]{:S(2)}, u32[]{:S(2)}) collective-permute-start(bf16[2,3,256]{2,0,1:T(2,128)(2,1)} %param.24), channel_id=1, source_target_pairs={{0,1},{1,0},{2,3},{3,2},{4,5},{5,4},{6,7},{7,6},{8,9},{9,8},{10,11... | collective-permute-start | bytes 9224 | tf_op jit(solution)/shard_map/ppermute | solution.py:474
  1.2 128.1 %collective-permute-start = (bf16[256]{0:T(256)(128)(2,1)}, bf16[256]{0:T(256)(128)(2,1)}, u32[]{:S(2)}, u32[]{:S(2)}) collective-permute-start(bf16[256]{0:T(256)(128)(2,1)} %param.32), channel_id=1, source_target_pairs={{0,1},{1,0},{2,3},{3,2},{4,5},{5,4},{6,7},{7,6},{8,9},{9,8},{10,11... | collective-permute-start | bytes 1544 | tf_op jit(solution)/shard_map/ppermute | solution.py:474
  4.4 118.3 %copy-start.23 = (f32[2,64]{1,0:T(2,128)}, f32[2,64]{1,0:T(2,128)S(1)}, u32[]{:S(2)}) copy-start(f32[2,64]{1,0:T(2,128)S(1)} %get-tuple-element.29) | copy-start | bytes 1540
  4.5 119.0 %copy-start.21 = (f32[2,64]{1,0:T(2,128)}, f32[2,64]{1,0:T(2,128)S(1)}, u32[]{:S(2)}) copy-start(f32[2,64]{1,0:T(2,128)S(1)} %get-tuple-element.30) | copy-start | bytes 1540
  4.5 118.3 %copy-start.25 = (pred[2,64]{1,0:T(4,128)(4,1)}, pred[2,64]{1,0:T(4,128)(4,1)S(1)}, u32[]{:S(2)}) copy-start(pred[2,64]{1,0:T(4,128)(4,1)S(1)} %get-tuple-element.26) | copy-start | bytes 388
  4.5 118.6 %copy-start.19 = (pred[2,64]{1,0:T(4,128)(4,1)}, pred[2,64]{1,0:T(4,128)(4,1)S(1)}, u32[]{:S(2)}) copy-start(pred[2,64]{1,0:T(4,128)(4,1)S(1)} %get-tuple-element.27) | copy-start | bytes 388
  4.5 119.0 %copy-start.26 = (pred[2,64]{1,0:T(4,128)(4,1)}, pred[2,64]{1,0:T(4,128)(4,1)S(1)}, u32[]{:S(2)}) copy-start(pred[2,64]{1,0:T(4,128)(4,1)S(1)} %get-tuple-element.28) | copy-start | bytes 388
  5.4 110.0 %copy-start.16 = (s32[2,64]{1,0:T(2,128)S(1)}, s32[2,64]{1,0:T(2,128)}, u32[]{:S(2)}) copy-start(s32[2,64]{1,0:T(2,128)} %param.38) | copy-start | bytes 1540
  112.6 4.4 %copy-start.10 = (bf16[2,128,256]{2,1,0:T(8,128)(2,1)S(1)}, bf16[2,128,256]{2,1,0:T(8,128)(2,1)}, u32[]{:S(2)}) copy-start(bf16[2,128,256]{2,1,0:T(8,128)(2,1)} %get-tuple-element.10) | copy-start | bytes 393220
  112.6 6.6 %copy-start.15 = (bf16[4,1024]{1,0:T(4,128)(2,1)S(1)}, bf16[4,1024]{1,0:T(4,128)(2,1)}, u32[]{:S(2)}) copy-start(bf16[4,1024]{1,0:T(4,128)(2,1)} %param.29) | copy-start | bytes 24580
  112.6 6.7 %copy-start.27 = (bf16[1024]{0:T(1024)(128)(2,1)S(1)}, bf16[1024]{0:T(1024)(128)(2,1)}, u32[]{:S(2)}) copy-start(bf16[1024]{0:T(1024)(128)(2,1)} %param.30) | copy-start | bytes 6148
  112.6 6.7 %copy-start.18 = (f32[16,128]{1,0:T(8,128)S(1)}, f32[16,128]{1,0:T(8,128)}, u32[]{:S(2)}) copy-start(f32[16,128]{1,0:T(8,128)} %get-tuple-element.9) | copy-start | bytes 24580
  112.6 6.8 %copy-start.29 = (f32[16]{0:T(128)S(1)}, f32[16]{0:T(128)}, u32[]{:S(2)}) copy-start(f32[16]{0:T(128)} %param.34) | copy-start | bytes 196
  112.6 6.8 %copy-start.30 = (s32[2]{0:T(128)S(1)}, s32[2]{0:T(128)}, u32[]{:S(2)}) copy-start(s32[2]{0:T(128)} %param.40) | copy-start | bytes 28
  112.6 6.8 %copy-start.28 = (s32[2,64]{1,0:T(2,128)S(1)}, s32[2,64]{1,0:T(2,128)}, u32[]{:S(2)}) copy-start(s32[2,64]{1,0:T(2,128)} %param.39) | copy-start | bytes 1540
  112.6 7.8 %copy-start.24 = (f32[16]{0:T(128)S(1)}, f32[16]{0:T(128)}, u32[]{:S(2)}) copy-start(f32[16]{0:T(128)} %param.33) | copy-start | bytes 196
  114.0 8.2 %copy-start.31 = (s32[2]{0:T(128)S(1)}, s32[2]{0:T(128)}, u32[]{:S(2)}) copy-start(s32[2]{0:T(128)} %param.41) | copy-start | bytes 28
  114.0 8.8 %copy-start.4 = (bf16[128,1024]{1,0:T(8,128)(2,1)S(1)}, bf16[128,1024]{1,0:T(8,128)(2,1)}, u32[]{:S(2)}) copy-start(bf16[128,1024]{1,0:T(8,128)(2,1)} %get-tuple-element.8) | copy-start | bytes 786436
  120.6 2.6 %copy-start.13 = (f32[2,64,16]{1,2,0:T(8,128)}, f32[2,64,16]{1,2,0:T(8,128)S(1)}, u32[]{:S(2)}) copy-start(f32[2,64,16]{1,2,0:T(8,128)S(1)} %compare_select_fusion) | copy-start | bytes 24580
  120.8 2.3 %copy-start.8 = (f32[2,64,16]{1,2,0:T(8,128)}, f32[2,64,16]{1,2,0:T(8,128)S(1)}, u32[]{:S(2)}) copy-start(f32[2,64,16]{1,2,0:T(8,128)S(1)} %fusion.48) | copy-start | bytes 24580
  123.1 1.5 copy-start.6
  126.4 9.0 %copy-start.3 = (f32[2,16,64,256]{3,2,1,0:T(8,128)S(1)}, f32[2,16,64,256]{3,2,1,0:T(8,128)}, u32[]{:S(2)}) copy-start(f32[2,16,64,256]{3,2,1,0:T(8,128)} %param.22) | copy-start | bytes 6291460
  129.3 6.0 %copy-start.12 = (f32[2,64,16]{1,2,0:T(8,128)S(1)}, f32[2,64,16]{1,2,0:T(8,128)}, u32[]{:S(2)}) copy-start(f32[2,64,16]{1,2,0:T(8,128)} %get-tuple-element.17) | copy-start | bytes 24580
  135.0 2.2 %copy-start.5 = (f32[2,64,16,64]{1,3,2,0:T(8,128)S(1)}, f32[2,64,16,64]{1,3,2,0:T(8,128)}, u32[]{:S(2)}) copy-start(f32[2,64,16,64]{1,3,2,0:T(8,128)} %copy.37) | copy-start | bytes 1572868
  135.0 2.2 %copy-start.9 = (f32[2,64,16]{1,2,0:T(8,128)S(1)}, f32[2,64,16]{1,2,0:T(8,128)}, u32[]{:S(2)}) copy-start(f32[2,64,16]{1,2,0:T(8,128)} %copy-done.8) | copy-start | bytes 24580
  135.0 2.2 %copy-start.14 = (f32[2,64,16]{1,2,0:T(8,128)S(1)}, f32[2,64,16]{1,2,0:T(8,128)}, u32[]{:S(2)}) copy-start(f32[2,64,16]{1,2,0:T(8,128)} %copy-done.13) | copy-start | bytes 24580
  135.0 2.2 %copy-start.17 = (pred[2,64,64]{2,1,0:T(8,128)(4,1)S(1)}, pred[2,64,64]{2,1,0:T(8,128)(4,1)}, u32[]{:S(2)}) copy-start(pred[2,64,64]{2,1,0:T(8,128)(4,1)} %copy.27) | copy-start | bytes 24580
  135.0 2.2 %copy-start.32 = (f32[16]{0:T(128)S(1)}, f32[16]{0:T(128)}, u32[]{:S(2)}) copy-start(f32[16]{0:T(128)} %param.35) | copy-start | bytes 196
  135.1 2.2 %copy-start.33 = (pred[2,64]{1,0:T(4,128)(4,1)S(1)}, pred[2,64]{1,0:T(4,128)(4,1)}, u32[]{:S(2)}) copy-start(pred[2,64]{1,0:T(4,128)(4,1)} %iota_compare_fusion.9) | copy-start | bytes 388
  137.3 3.4 %copy-start.11 = (f32[2,64,16]{1,2,0:T(8,128)S(1)}, f32[2,64,16]{1,2,0:T(8,128)}, u32[]{:S(2)}) copy-start(f32[2,64,16]{1,2,0:T(8,128)} %get-tuple-element.16) | copy-start | bytes 24580
  137.3 3.4 %copy-start.22 = (f32[2,16]{1,0:T(2,128)S(1)}, f32[2,16]{1,0:T(2,128)}, u32[]{:S(2)}) copy-start(f32[2,16]{1,0:T(2,128)} %exp.42) | copy-start | bytes 388
  140.7 6.3 %collective-permute-start.3 = (f32[2,64]{1,0:T(2,128)S(1)}, f32[2,64]{1,0:T(2,128)S(1)}, u32[]{:S(2)}, u32[]{:S(2)}) collective-permute-start(f32[2,64]{1,0:T(2,128)S(1)} %get-tuple-element.33), channel_id=1, source_target_pairs={{0,1},{1,0},{2,3},{3,2},{4,5},{5,4},{6,7},{7,6},{8,9},{9,8},{10,11... | collective-permute-start | bytes 1544 | tf_op jit(solution)/shard_map/ppermute | solution.py:474
  144.0 3.1 %copy-start.7 = (bf16[128,1024]{1,0:T(8,128)(2,1)S(1)}, bf16[128,1024]{1,0:T(8,128)(2,1)}, u32[]{:S(2)}) copy-start(bf16[128,1024]{1,0:T(8,128)(2,1)} %get-tuple-element.11) | copy-start | bytes 786436
  144.0 3.1 %copy-start.20 = (f32[1024]{0:T(1024)S(1)}, f32[1024]{0:T(1024)}, u32[]{:S(2)}) copy-start(f32[1024]{0:T(1024)} %param.36) | copy-start | bytes 12292
  144.0 4.3 %copy-start.1 = (bf16[4,1024,256]{2,1,0:T(8,128)(2,1)S(1)}, bf16[4,1024,256]{2,1,0:T(8,128)(2,1)}, u32[]{:S(2)}) copy-start(bf16[4,1024,256]{2,1,0:T(8,128)(2,1)} %get-tuple-element.12.wx) | copy-start | bytes 6291460
  148.3 1.6 copy-start.2

commit v2 on v1

v2 whole, which is shorter than its diff:
```python
import functools

import jax
import jax.numpy as jnp
from jax import lax
from jax.experimental import pallas as pl
from jax.experimental.pallas import tpu as pltpu
from jax.sharding import PartitionSpec as P

GROUP_WIDTH = 2048
MESH = pl.DeviceIdType.MESH
F32 = jnp.float32
BF16 = jnp.bfloat16
HIGHEST = lax.Precision.HIGHEST
TREE_PRECISION = HIGHEST
UNITS = (
    ("group", 0, 128, 128),
    ("inner", 0, 512, 256),
    ("inner", 256, 768, 256),
    ("gate", 0, 512, 256),
    ("gate", 256, 768, 256),
)


class Place:
    def __init__(self):
        self.r = lax.axis_index("req")
        self.h = lax.axis_index("head")
        self.y, self.x = self.r // 4, self.r % 4
        self.z, self.c = self.h // 2, self.h % 2

    def at(self, dy=0, dx=0, dz=0, dc=0):
        y, x = (self.y + dy) % 4, (self.x + dx) % 4
        z, c = (self.z + dz) % 8, (self.c + dc) % 2
        return (y * 4 + x, z * 2 + c)


def remote(src, dst, send, recv, device):
    return pltpu.make_async_remote_copy(
        src_ref=src, dst_ref=dst, send_sem=send, recv_sem=recv,
        device_id=device, device_id_type=MESH,
    )


def meet(devices, maybe=()):
    barrier = pltpu.get_barrier_semaphore()
    for device in devices:
        pl.semaphore_signal(barrier, inc=1, device_id=device, device_id_type=MESH)
    for device, here in maybe:
        @pl.when(here)
        def _():
            pl.semaphore_signal(barrier, inc=1, device_id=device, device_id_type=MESH)
    pl.semaphore_wait(barrier, len(devices) + sum(jnp.where(here, 1, 0) for _, here in maybe))


def dot(a, b, precision=None):
    return jnp.dot(a, b, preferred_element_type=F32, precision=precision)


def dot_nt(a, b, precision=None):
    return lax.dot_general(
        a, b, (((1,), (1,)), ((), ())), preferred_element_type=F32, precision=precision
    )


def dot_tn(a, b, precision=None):
    return lax.dot_general(
        a, b, (((0,), (0,)), ((), ())), preferred_element_type=F32, precision=precision
    )


def silu(u):
    return u / (1.0 + jnp.exp(-u))


def iota(shape, axis):
    return lax.broadcasted_iota(jnp.int32, shape, axis)


class Unit:
    def __init__(self, place, first, weight, column, width, tokens, out, bufs, send, recv):
        self.p, self.first = place, first
        self.a, self.b = (place.x, place.y) if first == "x" else (place.y, place.x)
        self.weight, self.column, self.width = weight, column, width
        self.tokens, self.out = tokens, out
        (self.s1, self.rf, self.s2p, self.s2m, self.rgp, self.rgm, self.q,
         self.s3, self.rh, self.s4p, self.s4m, self.rip, self.rim) = bufs
        self.send, self.recv = send, recv
        self.copies = {}

    def along(self, which, step):
        name = self.first if which == "a" else ("y" if self.first == "x" else "x")
        return self.p.at(dy=step) if name == "y" else self.p.at(dx=step)

    def part(self, dest_a, b):
        slot = 4 * b + dest_a if self.first == "x" else 4 * dest_a + b
        return dot(
            self.tokens[slot], self.weight[:, self.column : self.column + self.width]
        )

    def put(self, k, src, dst, which, step):
        copy = remote(src, dst, self.send.at[k], self.recv.at[k], self.along(which, step))
        copy.start()
        self.copies[k] = copy

    def stage1(self):
        far = (self.a + 2) % 4

        @pl.loop(0, 4)
        def _(b):
            self.s1[b] = self.part(far, b).astype(BF16)

        self.put(0, self.s1.at[0:2], self.rf.at[0:2], "a", 1)
        self.put(1, self.s1.at[2:4], self.rf.at[2:4], "a", -1)

    def stage2(self):
        self.copies[0].wait_recv()
        self.copies[1].wait_recv()
        up, down = (self.a + 1) % 4, (self.a + 3) % 4

        @pl.loop(0, 2)
        def _(b):
            self.s2p[b] = (self.part(up, b) + self.rf[b].astype(F32)).astype(BF16)
            self.s2p[b + 2] = self.part(up, b + 2).astype(BF16)
            self.s2m[b] = self.part(down, b).astype(BF16)
            self.s2m[b + 2] = (self.part(down, b + 2) + self.rf[b + 2].astype(F32)).astype(BF16)

        self.put(2, self.s2p, self.rgp, "a", 1)
        self.put(3, self.s2m, self.rgm, "a", -1)

    def stage3(self):
        self.copies[2].wait_recv()
        self.copies[3].wait_recv()

        @pl.loop(0, 4)
        def _(b):
            self.q[b] = self.part(self.a, b) + self.rgp[b].astype(F32) + self.rgm[b].astype(F32)

        self.s3[...] = self.q[(self.b + 2) % 4].astype(BF16)
        self.put(4, self.s3.at[0:64], self.rh.at[0:64], "b", 1)
        self.put(5, self.s3.at[64:128], self.rh.at[64:128], "b", -1)

    def stage4(self):
        self.copies[4].wait_recv()
        self.copies[5].wait_recv()
        up, down = (self.b + 1) % 4, (self.b + 3) % 4
        self.s4p[0:64] = (self.q[up, 0:64] + self.rh[0:64].astype(F32)).astype(BF16)
        self.s4p[64:128] = self.q[up, 64:128].astype(BF16)
        self.s4m[0:64] = self.q[down, 0:64].astype(BF16)
        self.s4m[64:128] = (self.q[down, 64:128] + self.rh[64:128].astype(F32)).astype(BF16)
        self.put(6, self.s4p, self.rip, "b", 1)
        self.put(7, self.s4m, self.rim, "b", -1)

    def stage5(self):
        self.copies[6].wait_recv()
        self.copies[7].wait_recv()
        total = self.q[self.b] + self.rip[...].astype(F32) + self.rim[...].astype(F32)
        self.out[0:128, self.column : self.column + self.width] = total.astype(BF16)

    def finish(self):
        for copy in self.copies.values():
            copy.wait_send()


def unit_scratch(width):
    def block(n, dtype=BF16):
        return pltpu.VMEM((n, 128, width), dtype)

    flat = pltpu.VMEM((128, width), BF16)
    return [block(4)] * 6 + [block(4, F32)] + [flat] * 6


def tree_setup(parents, reach, lags, sinner, sgroup, vinner, vgroup):
    lane = iota((1, 128), 1)
    own = jnp.concatenate((parents[0:1], parents[1:2]), axis=1)
    own = jnp.where(own < 0, -1, jnp.where(lane < 64, own, own + 64))
    parent = (iota((128, 128), 0) == own).astype(F32).T
    step = parent.astype(BF16)
    covered = (iota((128, 128), 0) == iota((128, 128), 1)).astype(F32) + parent
    for _ in range(6):
        half = covered.astype(BF16)
        covered = jnp.minimum(dot(half, half), 1.0)
    reach[...] = covered
    depth = jnp.sum(covered, axis=1, keepdims=True).astype(jnp.int32) - 1
    row, col = iota((128, 128), 0), iota((128, 128), 1)
    same = (col < 6) & (row // 64 == col // 3)
    ancestor = step
    for k in range(1, 4):
        if k > 1:
            ancestor = dot(ancestor, step).astype(BF16)
        prior = same & (k > depth) & (col % 3 == 3 - k + depth)
        lags[128 * (k - 1) : 128 * k, 0:128] = ancestor
        lags[128 * (k - 1) : 128 * k, 128:256] = prior.astype(F32).astype(BF16)
    for prior, values in ((sinner, vinner), (sgroup, vgroup)):
        width = values.shape[1]
        six = jnp.concatenate((prior[0].astype(F32), prior[1].astype(F32)), axis=0)
        six = jnp.concatenate((six, jnp.zeros((2, width), F32)), axis=0)
        values[128:256] = jnp.concatenate((six, jnp.zeros((120, width), F32)), axis=0).astype(BF16)


def tree_conv(values, lags, taps, bias, lo, width):
    at = slice(lo, lo + width)
    earlier = dot(lags[...], values[:, at])
    taps = taps[:, at].astype(F32)
    total = bias + taps[3:4] * values[0:128, at].astype(F32)
    for k in range(1, 4):
        total = total + taps[3 - k : 4 - k] * earlier[128 * (k - 1) : 128 * k]
    return silu(total)


def as_column(row):
    n = row.shape[1]
    return jnp.sum(jnp.where(iota((n, n), 0) == iota((n, n), 1), row, 0.0), axis=1, keepdims=True)


def tree_steps(sums, params, reach, path, plen, sizes, cum_t, cum, leaf_w, leaf_e):
    raw = sums.astype(BF16).astype(F32) + as_column(params[3:4, 0:16])
    size = jnp.maximum(raw, 0.0) + jnp.log1p(jnp.exp(-jnp.abs(raw)))
    log_decay = -as_column(params[4:5, 0:16]) * size
    total = dot_nt(log_decay, reach[...], HIGHEST)
    sizes[...] = size
    cum_t[...] = total
    cum[...] = total.T
    weights = jnp.zeros((16, 128), F32)
    for q in range(2):
        last = iota((1, 64), 1) == plen[q] - 1
        leaf = jnp.sum(jnp.where(last, path[q : q + 1], 0), axis=1, keepdims=True) + 64 * q
        here = (iota((1, 128), 1) == leaf).astype(F32)
        above = dot(here.astype(BF16), reach[...].astype(BF16))
        at_leaf = jnp.sum(here * total, axis=1, keepdims=True)
        weights = weights + jnp.where(above > 0, jnp.exp(jnp.minimum(at_leaf - total, 0.0)), 0.0)
        leaf_e[:, 128 * q : 128 * q + 128] = jnp.broadcast_to(jnp.exp(at_leaf), (16, 128))
    leaf_w[...] = (weights * size).T


def tree_outputs(values, states, channels, sizes, cum_t, cum, reach, params, tsize, out):
    for q in range(2):
        rows = slice(64 * q, 64 * q + 64)
        out[rows] = dot_nt(values[1, rows], states[q], TREE_PRECISION)
    meet_bc = dot_nt(values[1], values[0], TREE_PRECISION)
    linked = reach[...] > 0
    lane = iota((128, 128), 1) < 64
    row = iota((128, 1), 0)
    valid = jnp.where(row < 64, row, row - 64) < jnp.where(row < 64, tsize[0], tsize[1])
    for pair in range(8):
        at = slice(128 * pair, 128 * pair + 128)
        x = channels[:, at]
        mixes, grown, skips = [], [], []
        for head in (2 * pair, 2 * pair + 1):
            column, across = cum[:, head : head + 1], cum_t[head : head + 1]
            decay = jnp.where(linked, jnp.exp(jnp.minimum(column - across, 0.0)), 0.0)
            mixes.append(decay * meet_bc * sizes[head : head + 1])
            grown.append(jnp.exp(column))
            skips.append(params[5:6, head : head + 1])
        both = dot(
            jnp.concatenate(mixes, axis=1),
            jnp.concatenate((jnp.where(lane, x, 0.0), jnp.where(lane, 0.0, x)), axis=0),
            TREE_PRECISION,
        )
        total = both + jnp.where(lane, grown[0], grown[1]) * out[:, at]
        total = total + jnp.where(lane, skips[0], skips[1]) * x
        out[:, at] = jnp.where(valid, total, 0.0)


def advance(q, part, states, channels, values, leaf_w, leaf_e):
    rows = slice(64 * q, 64 * q + 64)
    lane = iota((64, 128), 1) < 64
    for pair in range(4 * part, 4 * part + 4):
        at = slice(128 * pair, 128 * pair + 128)
        weight = jnp.where(
            lane, leaf_w[rows, 2 * pair : 2 * pair + 1], leaf_w[rows, 2 * pair + 1 : 2 * pair + 2]
        )
        added = dot_tn(channels[rows, at] * weight, values[0, rows], TREE_PRECISION)
        for j in range(2):
            head = 2 * pair + j
            kept = leaf_e[head : head + 1, 128 * q : 128 * q + 1]
            block = slice(64 * head, 64 * head + 64)
            states[q, block] = kept * states[q, block] + added[64 * j : 64 * j + 64]


ORDER = (
    (1, 0), (1, 1), (2, 0), (1, 2), (2, 1), (3, 0), (1, 3), (2, 2), (3, 1), (4, 0), (1, 4),
    (3, 2), (4, 1), (5, 0), (2, 3), (4, 2), (5, 1), (2, 4), (5, 2),
    (3, 3), (3, 4), (4, 3), (4, 4), (5, 3), (5, 4),
)


def mixer_kernel(*refs):
    (tok, state, sinner, sgroup, wgate_hbm, winner_hbm, wgroup_hbm, wstep, tinner, tgroup,
     params, wout, parents, path, plen, tsize, mixed, next_state,
     tg, st, sr, wst, wgate, winner, wgroup, states, wx, wy,
     reach, lags, vinner, vgroup, gate, values, channels, sizes, cum_t, cum, leaf_w, leaf_e,
     outs_f, sq_s, sq_r, norm,
     nx, ny, own, sent, got, zsend_p, zsend_m, zgot_p, zgot_m, fin, land,
     loads, turn_s, turn_r, local, zs, zr, cs, cr, ss, sr_sem, os, orr, gs, gr, us, ur,
     bc_s, bc_r, sq_ss, sq_rs, ns, nr, ks, kr, vs, vr, fs, fr, store) = refs[:84]
    bufs = refs[84:]
    p = Place()
    r, h, y, x, z, c = p.r, p.h, p.y, p.x, p.z, p.c
    hy, hx = h // 4, h % 4
    other = hy * 4 + hx
    moved = r != h
    goal = ((hy * 4 + x, y * 4 + hx), (y * 4 + hx, hy * 4 + x))
    away = (hy != y, hx != x)

    fetch = []
    for k, (src, dst) in enumerate(
        ((wgroup_hbm, wgroup), (winner_hbm, winner), (wgate_hbm, wgate), (state, states))
    ):
        fetch.append(pltpu.make_async_copy(src, dst, loads.at[k]))
        fetch[-1].start()

    meet(
        [((r + j) % 16, h) for j in range(1, 16)] + [p.at(dz=1), p.at(dz=-1), p.at(dc=1)],
        [((other, r), moved), (goal[0], away[0]), (goal[1], away[1])],
    )
    turn = remote(tok, tg.at[r], turn_s, turn_r, (other, r))
    keep_tok = pltpu.make_async_copy(tok, tg.at[r], local)

    @pl.when(moved)
    def _():
        turn.start()

    @pl.when(jnp.logical_not(moved))
    def _():
        keep_tok.start()

    near, keeps = [], []
    for k, (ax, full, lo, d) in enumerate(
        (("x", wx, 0, 1), ("x", wx, 0, -1), ("y", wy, 256, 1), ("y", wy, 256, -1))
    ):
        me = x if ax == "x" else y
        peer = p.at(dx=d) if ax == "x" else p.at(dy=d)
        copy = remote(wout.at[:, lo : lo + 256], full.at[me], os.at[k], orr.at[k], peer)
        copy.start()
        near.append((copy, ax, full, d, me, peer))
        if d == 1:
            keeps.append(pltpu.make_async_copy(wout.at[:, lo : lo + 256], full.at[me], loads.at[4 + k // 2]))
            keeps[-1].start()

    tree_setup(parents, reach, lags, sinner, sgroup, vinner, vgroup)
    wst[...] = wstep[...].astype(F32).T.astype(BF16)

    @pl.when(moved)
    def _():
        turn.wait()

    @pl.when(jnp.logical_not(moved))
    def _():
        keep_tok.wait()

    def block(dz):
        return 2 * ((z + dz) % 8) + c

    cores, ring = [], []

    def to_core(dz):
        k = len(cores)
        copy = remote(tg.at[block(dz)], tg.at[block(dz)], cs.at[k], cr.at[k], p.at(dc=1))
        copy.start()
        cores.append(copy)

    def hop(dz, d, lo, n):
        k = len(ring)
        ref = tg.at[block(dz), lo : lo + n]
        copy = remote(ref, ref, zs.at[k], zr.at[k], p.at(dz=d))
        copy.start()
        ring.append(copy)
        return copy

    plus, minus = hop(0, 1, 0, 128), hop(0, -1, 0, 128)
    to_core(0)
    for s in range(1, 4):
        rows = 128 if s < 3 else 64
        plus.wait_recv()
        plus = hop(-s, 1, 0, rows)
        minus.wait_recv()
        minus = hop(s, -1, 128 - rows, rows)
        to_core(-s)
        to_core(s)
    plus.wait_recv()
    minus.wait_recv()
    to_core(4)
    far = []
    for k, (copy, ax, full, d, me, peer) in enumerate(near):
        copy.wait_recv()
        lo = 0 if d == 1 else 512
        ref = full.at[(me - d) % 4, lo : lo + 512]
        far.append(remote(ref, ref, gs.at[k], gr.at[k], peer))
        far[-1].start()
    for copy in cores:
        copy.wait_recv()
    for copy in fetch[:3]:
        copy.wait()

    @pl.loop(0, 16)
    def _(k):
        st[k] = dot_nt(wst[...], tg[k])

    @pl.loop(1, 16)
    def _(j):
        to = (r + j) % 16
        remote(st.at[to], sr.at[j], ss, sr_sem, (to, h)).start()

    sources = {"group": wgroup, "inner": winner, "gate": wgate}
    results = {"group": vgroup, "inner": vinner, "gate": gate}
    units = []
    for i, (name, xcol, ycol, width) in enumerate(UNITS):
        pair = []
        for j, (first, col) in enumerate((("x", xcol), ("y", ycol))):
            n = 2 * i + j
            pair.append(Unit(p, first, sources[name], col, width, tg, results[name],
                             bufs[13 * n : 13 * n + 13], us.at[n], ur.at[n]))
        units.append(pair)
    swap = remote(values.at[c], values.at[c], bc_s, bc_r, p.at(dc=1))
    tail = sr.at[1:16]
    for stage, unit in ORDER:
        for one in units[unit]:
            getattr(one, "stage%d" % stage)()
        if (stage, unit) == (5, 0):
            values[c] = tree_conv(vgroup, lags, tgroup, params[2:3, 0:256], 0, 256)
            swap.start()
            pltpu.make_async_copy(tail, tail, sr_sem).wait()
            sums = st[r]
            for j in range(1, 16):
                sums = sums + sr[j]
            tree_steps(sums, params, reach, path, plen, sizes, cum_t, cum, leaf_w, leaf_e)
        if stage == 5 and unit in (1, 2):
            for one in units[unit]:
                lo = one.column
                channels[:, lo : lo + 256] = tree_conv(
                    vinner, lags, tinner, params[1:2, lo : lo + 256], lo, 256
                )
        if (stage, unit) == (5, 2):
            swap.wait_recv()
            fetch[3].wait()
            tree_outputs(values, states, channels, sizes, cum_t, cum, reach, params, tsize, outs_f)

    squares = jnp.zeros((128, 128), F32)
    for k in range(8):
        at = slice(128 * k, 128 * k + 128)
        gated = outs_f[:, at] * silu(gate[:, at].astype(F32))
        outs_f[:, at] = gated
        squares = squares + gated * gated
    sq_s[...] = squares
    trade = remote(sq_s, sq_r, sq_ss, sq_rs, p.at(dc=1))
    trade.start()
    trade.wait_recv()
    mean = jnp.sum(sq_s[...] + sq_r[...], axis=1, keepdims=True) / GROUP_WIDTH
    norm[...] = (outs_f[...] * lax.rsqrt(mean + 1e-05) * params[0:1]).astype(BF16)

    spread = []
    for d in (1, 3, 2):
        for full, peer in ((ny.at[y], p.at(dy=d)), (nx.at[x], p.at(dx=d))):
            k = len(spread)
            copy = remote(norm, full, ns.at[k], nr.at[k], peer)
            copy.start()
            spread.append(copy)
    nx[x] = norm[...]
    ny[y] = norm[...]
    for copy in keeps:
        copy.wait()
    for copy in far:
        copy.wait_recv()

    def shard(zz, cc):
        s = 2 * zz + cc
        i, j = s // 4, s % 4
        return dot(ny[i], wx[j]), dot(nx[j], wy[i])

    for copy in spread:
        copy.wait_recv()

    @pl.loop(0, 8)
    def _(zz):
        left, right = shard(zz, 1 - c)
        sent[zz, 0] = left.astype(BF16)
        sent[zz, 1] = right.astype(BF16)

    pass_on = remote(sent, got, ks, kr, p.at(dc=1))
    pass_on.start()

    @pl.loop(0, 8)
    def _(zz):
        left, right = shard(zz, c)
        own[zz, 0] = left
        own[zz, 1] = right

    pass_on.wait_recv()

    def mine(dz, half):
        zz = (z + dz) % 8
        return own[zz, half] + got[zz, half].astype(F32)

    moves = []

    def move(src, dst, d):
        k = len(moves)
        copy = remote(src, dst, vs.at[k], vr.at[k], p.at(dz=d))
        copy.start()
        moves.append(copy)
        return copy

    stores = []

    def grow(k):
        q, part = k // 2, k % 2
        advance(q, part, states, channels, values, leaf_w, leaf_e)
        ref = slice(512 * part, 512 * part + 512)
        copy = pltpu.make_async_copy(states.at[q, ref], next_state.at[q, ref], store.at[k])
        copy.start()
        stores.append(copy)

    zsend_p[0, 0] = mine(4, 0).astype(BF16)
    plus = move(zsend_p.at[0, 0], zgot_p.at[0, 0], 1)
    zsend_m[0, 1] = mine(4, 1).astype(BF16)
    minus = move(zsend_m.at[0, 1], zgot_m.at[0, 1], -1)
    for s in (1, 2, 3):
        grow(s - 1)
        plus.wait_recv()
        zsend_p[s, 0] = (mine(4 - s, 0) + zgot_p[s - 1, 0].astype(F32)).astype(BF16)
        if s == 1:
            zsend_p[s, 1] = mine(4 - s, 1).astype(BF16)
        else:
            zsend_p[s, 1] = (mine(4 - s, 1) + zgot_p[s - 1, 1].astype(F32)).astype(BF16)
        plus = move(zsend_p.at[s], zgot_p.at[s], 1)
        minus.wait_recv()
        if s == 1:
            zsend_m[s, 0] = mine(s - 4, 0).astype(BF16)
        else:
            zsend_m[s, 0] = (mine(s - 4, 0) + zgot_m[s - 1, 0].astype(F32)).astype(BF16)
        zsend_m[s, 1] = (mine(s - 4, 1) + zgot_m[s - 1, 1].astype(F32)).astype(BF16)
        minus = move(zsend_m.at[s], zgot_m.at[s], -1)
    grow(3)
    plus.wait_recv()
    minus.wait_recv()

    def home(half):
        return remote(fin.at[half], land.at[half], fs.at[half], fr.at[half], goal[half])

    for half in (0, 1):
        fin[half] = (
            mine(0, half) + zgot_p[3, half].astype(F32) + zgot_m[3, half].astype(F32)
        ).astype(BF16)

        @pl.when(away[half])
        def _():
            home(half).start()

        @pl.when(jnp.logical_not(away[half]))
        def _():
            land[half] = fin[half]

    for pair in units:
        for one in pair:
            one.finish()
    pltpu.make_async_copy(tail, tail, ss).wait()
    for copy in cores + ring + [one[0] for one in near] + far + [swap, trade, pass_on] + spread + moves:
        copy.wait_send()
    for copy in stores:
        copy.wait()
    for half in (0, 1):

        @pl.when(away[half])
        def _():
            home(half).wait()

        mixed[:, 256 * half : 256 * half + 256] = land[half]


def mixer(*args):
    vmem = pl.BlockSpec(memory_space=pltpu.VMEM)
    smem = pl.BlockSpec(memory_space=pltpu.SMEM)
    hbm = pl.BlockSpec(memory_space=pl.ANY)
    dma = pltpu.SemaphoreType.DMA

    def flat(*shape):
        return pltpu.VMEM(shape, F32)

    def half(*shape):
        return pltpu.VMEM(shape, BF16)

    scratch = [
        half(16, 128, 512), flat(16, 16, 128), flat(16, 16, 128), half(16, 512),
        half(512, 1024), half(512, 1024), half(512, 256), flat(2, 1024, 256),
        half(4, 1024, 256), half(4, 1024, 256),
        flat(128, 128), half(384, 256), half(256, 1024), half(256, 256), half(128, 1024),
        flat(2, 128, 256), flat(128, 1024), flat(16, 128), flat(16, 128), flat(128, 16),
        flat(128, 16), flat(16, 256), flat(128, 1024), flat(128, 128), flat(128, 128),
        half(128, 1024),
        half(4, 128, 1024), half(4, 128, 1024), flat(8, 2, 128, 256),
        half(8, 2, 128, 256), half(8, 2, 128, 256),
        half(4, 2, 128, 256), half(4, 2, 128, 256), half(4, 2, 128, 256), half(4, 2, 128, 256),
        half(2, 128, 256), half(2, 128, 256),
        dma((6,)), dma, dma, dma, dma((8,)), dma((8,)), dma((8,)), dma((8,)), dma, dma,
        dma((4,)), dma((4,)), dma((4,)), dma((4,)),
        dma((2 * len(UNITS), 8)), dma((2 * len(UNITS), 8)),
        dma, dma, dma, dma, dma((6,)), dma((6,)), dma, dma, dma((8,)), dma((8,)),
        dma((2,)), dma((2,)), dma((4,)),
    ]
    for _, _, _, width in UNITS:
        scratch += unit_scratch(width) * 2
    shape = jax.ShapeDtypeStruct
    return pl.pallas_call(
        mixer_kernel,
        name="mixer",
        out_shape=(shape((128, 512), BF16), shape((2, 1024, 256), F32)),
        in_specs=[vmem, hbm, vmem, vmem, hbm, hbm, hbm, vmem, vmem, vmem, vmem, hbm, vmem, vmem, smem, smem],
        out_specs=(vmem, hbm),
        scratch_shapes=scratch,
        compiler_params=pltpu.CompilerParams(
            collective_id=0, has_side_effects=True, vmem_limit_bytes=58 * 2**20
        ),
    )(*args)


def on_device(
    tokens, prior_state, conv_inner_state, conv_group_state, gate_weight, inner_weight,
    group_weight, step_weight, conv_inner_weight, conv_inner_bias, conv_group_weight,
    conv_group_bias, step_bias, decay_rate, skip_gain, norm_gain, out_weight, parents,
    accepted_path, path_length, tree_size,
):
    rows = (norm_gain, conv_inner_bias, conv_group_bias, step_bias, decay_rate, skip_gain)
    params = jnp.stack([jnp.pad(row.astype(F32), (0, 1024 - row.shape[0])) for row in rows])
    mixed, state = mixer(
        tokens, prior_state.reshape(2, 1024, 256), conv_inner_state, conv_group_state,
        gate_weight, inner_weight, group_weight, step_weight, conv_inner_weight,
        conv_group_weight, params, out_weight, parents, accepted_path, path_length, tree_size,
    )
    return mixed, state.reshape(prior_state.shape)


def solution(mesh):
    in_specs = (
        P("req", "head"),
        P("req", "head", None, None),
        P("req", None, "head"),
        P("req", None, "head"),
        P("req", "head"),
        P("req", "head"),
        P("req", "head"),
        P("req", "head"),
        P(None, "head"),
        P("head"),
        P(None, "head"),
        P("head"),
        P("head"),
        P("head"),
        P("head"),
        P("head"),
        P("head", "req"),
        P("req", None),
        P("req", None),
        P("req"),
        P("req"),
    )
    out_specs = (P("req", "head"), P("req", "head", None, None))
    return jax.shard_map(
        on_device, mesh=mesh, in_specs=in_specs, out_specs=out_specs, check_vma=False
    )
```

time: 199 us -> 167 us (0.84)
  matrix products: 24.8 us -> 0 us
  other arithmetic: 5.84 us -> 1.34 us
  Pallas kernels: 154 us -> 151 us
    dot_general x28 -> x0, matrix products: 24.8 us -> none  [the longest x6 6.22 us: tree_conv(): jnp.einsum('rij,rjc->ric', ancestor_step, values, precision=HIGHEST_PRECI...]
    unnamed x69 -> x5, local copies, waits for them, and re-layouts: 2.41 us -> 8.76 us
    pallas_call x2 -> x1, Pallas kernels: 154 us -> 151 us  [mixer(): pl.pallas_call(mixer_kernel, name='mixer', out_shape=(shape((128, 512), B...]
    convert_element_type x6 -> x0, other arithmetic: 2.76 us -> none  [the longest x1 1.24 us: on_device(): (gated * lax.rsqrt(mean_square + 1e-05)[..., None] * norm_gain).astype(jn...]
    reshape x2 -> x0, local copies, waits for them, and re-layouts: 2.63 us -> none  [the longest x1 1.52 us: on_device(): heads_x = channels.reshape(request_count, node_count, heads_local, HEAD_DIM)]
  transfers between devices with their start and end apart: 4 -> 0, of which waited for: 0 -> 0; matrix products, arithmetic and copies ran while one was open for 14% -> 0% of each run, Pallas kernels for 54% -> 0%
where the time goes in v2:
time: 167 us; the launch traced here: 165 us
  Pallas kernels  151 us (90%)
  local copies, waits for them, and re-layouts  12.1 us (7%)
    pallas_call x1, Pallas kernels, mixer(): pl.pallas_call(mixer_kernel, name='mixer', out_shape=(shape((128, 512), B...  151 us
    unnamed x5, local copies, waits for them, and re-layouts  8.76 us

profile of v2, /device:TPU:16, one launch (start us, length us, event | category | flops | bytes accessed | tf_op | source)
XLA Modules:
  0.0 165.0 jit_solution(11851513801002380173)
XLA Ops:
  0.6 1.3 copy.24.refs_3_
  1.9 0.7 stack.36
  2.6 0.7 pad_convert_fusion
  3.3 0.7 pad.16
  3.9 0.7 pad.17
  4.6 0.7 pad.18
  5.2 1.3 stack.35.refs_10_
  6.6 1.3 copy.23.refs_2_
  7.9 1.5 copy.25.refs_7_
  9.4 151.0 %mixer.1 = (bf16[128,512]{1,0:T(8,128)(2,1)}, f32[2,1024,256]{2,1,0:T(8,128)}) custom-call(bf16[128,512]{1,0:T(8,128)(2,1)} %refs_0_.1, f32[2,1024,256]{2,1,0:T(8,128)} %bitcast.8, bf16[2,3,1024]{2,1,0:T(4,128)(2,1)} %copy.23.refs_2_, bf16[2,3,256]{2,1,0:T(4,128)(2,1)} %copy.24.refs_3_, bf16[512,1024]{1,0:T(8,128)(2,1)} %refs_4_.1, ...), custom_call_target="tpu_custom_call" | custom-call | tf_op jit(solution)/shard_map/mixer/pallas_call | solution.py:604
  160.3 1.6 copy.28
  161.9 3.1 %copy.29 = f32[2,16,64,256]{3,2,1,0:T(8,128)} copy(f32[2,16,64,256]{3,2,1,0:T(8,128)} %bitcast.9) | data formatting | bytes 4194304

commit v3 on v2

--- a/solution.py
+++ b/solution.py
@@ -92,11 +92,10 @@
         name = self.first if which == "a" else ("y" if self.first == "x" else "x")
         return self.p.at(dy=step) if name == "y" else self.p.at(dx=step)
 
-    def part(self, dest_a, b):
-        slot = 4 * b + dest_a if self.first == "x" else 4 * dest_a + b
-        return dot(
-            self.tokens[slot], self.weight[:, self.column : self.column + self.width]
-        )
+    def part(self, dest_a):
+        slots = [4 * b + dest_a if self.first == "x" else 4 * dest_a + b for b in range(4)]
+        rows = jnp.concatenate([self.tokens[slot] for slot in slots], axis=0)
+        return dot(rows, self.weight[:, self.column : self.column + self.width])
 
     def put(self, k, src, dst, which, step):
         copy = remote(src, dst, self.send.at[k], self.recv.at[k], self.along(which, step))
@@ -104,38 +103,30 @@
         self.copies[k] = copy
 
     def stage1(self):
-        far = (self.a + 2) % 4
-
-        @pl.loop(0, 4)
-        def _(b):
-            self.s1[b] = self.part(far, b).astype(BF16)
-
+        far = self.part((self.a + 2) % 4).astype(BF16)
+        for b in range(4):
+            self.s1[b] = far[128 * b : 128 * b + 128]
         self.put(0, self.s1.at[0:2], self.rf.at[0:2], "a", 1)
         self.put(1, self.s1.at[2:4], self.rf.at[2:4], "a", -1)
 
     def stage2(self):
-        self.copies[0].wait_recv()
-        self.copies[1].wait_recv()
-        up, down = (self.a + 1) % 4, (self.a + 3) % 4
-
-        @pl.loop(0, 2)
-        def _(b):
-            self.s2p[b] = (self.part(up, b) + self.rf[b].astype(F32)).astype(BF16)
-            self.s2p[b + 2] = self.part(up, b + 2).astype(BF16)
-            self.s2m[b] = self.part(down, b).astype(BF16)
-            self.s2m[b + 2] = (self.part(down, b + 2) + self.rf[b + 2].astype(F32)).astype(BF16)
-
-        self.put(2, self.s2p, self.rgp, "a", 1)
-        self.put(3, self.s2m, self.rgm, "a", -1)
+        for k, step, to, whole in ((0, 1, self.s2p, self.rgp), (1, -1, self.s2m, self.rgm)):
+            terms = self.part((self.a + step) % 4)
+            self.copies[k].wait_recv()
+            for b in range(4):
+                term = terms[128 * b : 128 * b + 128]
+                if b // 2 == k:
+                    term = term + self.rf[b].astype(F32)
+                to[b] = term.astype(BF16)
+            self.put(2 + k, to, whole, "a", step)
 
     def stage3(self):
+        terms = self.part(self.a)
         self.copies[2].wait_recv()
         self.copies[3].wait_recv()
-
-        @pl.loop(0, 4)
-        def _(b):
-            self.q[b] = self.part(self.a, b) + self.rgp[b].astype(F32) + self.rgm[b].astype(F32)
-
+        for b in range(4):
+            term = terms[128 * b : 128 * b + 128]
+            self.q[b] = term + self.rgp[b].astype(F32) + self.rgm[b].astype(F32)
         self.s3[...] = self.q[(self.b + 2) % 4].astype(BF16)
         self.put(4, self.s3.at[0:64], self.rh.at[0:64], "b", 1)
         self.put(5, self.s3.at[64:128], self.rh.at[64:128], "b", -1)
@@ -170,7 +161,7 @@
     return [block(4)] * 6 + [block(4, F32)] + [flat] * 6
 
 
-def tree_setup(parents, reach, lags, sinner, sgroup, vinner, vgroup):
+def tree_setup(parents, reach, lags, priors):
     lane = iota((1, 128), 1)
     own = jnp.concatenate((parents[0:1], parents[1:2]), axis=1)
     own = jnp.where(own < 0, -1, jnp.where(lane < 64, own, own + 64))
@@ -191,10 +182,11 @@
         prior = same & (k > depth) & (col % 3 == 3 - k + depth)
         lags[128 * (k - 1) : 128 * k, 0:128] = ancestor
         lags[128 * (k - 1) : 128 * k, 128:256] = prior.astype(F32).astype(BF16)
-    for prior, values in ((sinner, vinner), (sgroup, vgroup)):
+    for prior, values in priors:
         width = values.shape[1]
-        six = jnp.concatenate((prior[0].astype(F32), prior[1].astype(F32)), axis=0)
-        six = jnp.concatenate((six, jnp.zeros((2, width), F32)), axis=0)
+        both = [prior[k].astype(F32) for k in range(3)]
+        six = [both[k][q : q + 1] for q in range(2) for k in range(3)]
+        six = jnp.concatenate(six + [jnp.zeros((2, width), F32)], axis=0)
         values[128:256] = jnp.concatenate((six, jnp.zeros((120, width), F32)), axis=0).astype(BF16)
 
 
@@ -213,10 +205,10 @@
     return jnp.sum(jnp.where(iota((n, n), 0) == iota((n, n), 1), row, 0.0), axis=1, keepdims=True)
 
 
-def tree_steps(sums, params, reach, path, plen, sizes, cum_t, cum, leaf_w, leaf_e):
-    raw = sums.astype(BF16).astype(F32) + as_column(params[3:4, 0:16])
+def tree_steps(sums, bias, rate, reach, path, plen, sizes, cum_t, cum, leaf_w, leaf_e):
+    raw = sums.astype(BF16).astype(F32) + as_column(bias[...])
     size = jnp.maximum(raw, 0.0) + jnp.log1p(jnp.exp(-jnp.abs(raw)))
-    log_decay = -as_column(params[4:5, 0:16]) * size
+    log_decay = -as_column(rate[...]) * size
     total = dot_nt(log_decay, reach[...], HIGHEST)
     sizes[...] = size
     cum_t[...] = total
@@ -233,7 +225,7 @@
     leaf_w[...] = (weights * size).T
 
 
-def tree_outputs(values, states, channels, sizes, cum_t, cum, reach, params, tsize, out):
+def tree_outputs(values, states, channels, sizes, cum_t, cum, reach, gain, tsize, out):
     for q in range(2):
         rows = slice(64 * q, 64 * q + 64)
         out[rows] = dot_nt(values[1, rows], states[q], TREE_PRECISION)
@@ -251,7 +243,7 @@
             decay = jnp.where(linked, jnp.exp(jnp.minimum(column - across, 0.0)), 0.0)
             mixes.append(decay * meet_bc * sizes[head : head + 1])
             grown.append(jnp.exp(column))
-            skips.append(params[5:6, head : head + 1])
+            skips.append(gain[0:1, head : head + 1])
         both = dot(
             jnp.concatenate(mixes, axis=1),
             jnp.concatenate((jnp.where(lane, x, 0.0), jnp.where(lane, 0.0, x)), axis=0),
@@ -286,20 +278,22 @@
 
 
 def mixer_kernel(*refs):
-    (tok, state, sinner, sgroup, wgate_hbm, winner_hbm, wgroup_hbm, wstep, tinner, tgroup,
-     params, wout, parents, path, plen, tsize, mixed, next_state,
-     tg, st, sr, wst, wgate, winner, wgroup, states, wx, wy,
+    (tok, state, sinner, sgroup, wgate_hbm, winner_hbm, wgroup_hbm, wst, tinner, tgroup,
+     biases, step_bias, decay_rate, skip_gain, norm_gain, wout, parents, path, plen, tsize,
+     mixed, next_state,
+     tg, st, sr, wgate, winner, wgroup, states, wx, wy,
      reach, lags, vinner, vgroup, gate, values, channels, sizes, cum_t, cum, leaf_w, leaf_e,
-     outs_f, sq_s, sq_r, norm,
+     outs_f, sq_s, sq_r, inv, inv_x, inv_y, norm,
      nx, ny, own, sent, got, zsend_p, zsend_m, zgot_p, zgot_m, fin, land,
      loads, turn_s, turn_r, local, zs, zr, cs, cr, ss, sr_sem, os, orr, gs, gr, us, ur,
-     bc_s, bc_r, sq_ss, sq_rs, ns, nr, ks, kr, vs, vr, fs, fr, store) = refs[:84]
-    bufs = refs[84:]
+     bc_s, bc_r, sq_ss, sq_rs, is_, ir, ns, nr, ks, kr, vs, vr, fs, fr, store) = refs[:92]
+    bufs = refs[92:]
     p = Place()
     r, h, y, x, z, c = p.r, p.h, p.y, p.x, p.z, p.c
     hy, hx = h // 4, h % 4
-    other = hy * 4 + hx
-    moved = r != h
+    turn_to = (h, 2 * ((z + r // 2) % 8) + r % 2)
+    turn_from = (2 * ((z - r // 2) % 8) + c, r)
+    moved = jnp.logical_or(turn_to[0] != r, turn_to[1] != h)
     goal = ((hy * 4 + x, y * 4 + hx), (y * 4 + hx, hy * 4 + x))
     away = (hy != y, hx != x)
 
@@ -312,9 +306,9 @@
 
     meet(
         [((r + j) % 16, h) for j in range(1, 16)] + [p.at(dz=1), p.at(dz=-1), p.at(dc=1)],
-        [((other, r), moved), (goal[0], away[0]), (goal[1], away[1])],
+        [(turn_from, moved), (goal[0], away[0]), (goal[1], away[1])],
     )
-    turn = remote(tok, tg.at[r], turn_s, turn_r, (other, r))
+    turn = remote(tok, tg.at[r], turn_s, turn_r, turn_to)
     keep_tok = pltpu.make_async_copy(tok, tg.at[r], local)
 
     @pl.when(moved)
@@ -324,6 +318,16 @@
     @pl.when(jnp.logical_not(moved))
     def _():
         keep_tok.start()
+
+    tree_setup(parents, reach, lags, ((sinner, vinner), (sgroup, vgroup)))
+
+    @pl.when(moved)
+    def _():
+        turn.wait()
+
+    @pl.when(jnp.logical_not(moved))
+    def _():
+        keep_tok.wait()
 
     near, keeps = [], []
     for k, (ax, full, lo, d) in enumerate(
@@ -331,28 +335,22 @@
     ):
         me = x if ax == "x" else y
         peer = p.at(dx=d) if ax == "x" else p.at(dy=d)
-        copy = remote(wout.at[:, lo : lo + 256], full.at[me], os.at[k], orr.at[k], peer)
-        copy.start()
-        near.append((copy, ax, full, d, me, peer))
+        first = 0 if d == 1 else 512
+        for n, rows in enumerate((first, 512 - first)):
+            copy = remote(
+                wout.at[rows : rows + 512, lo : lo + 256], full.at[me, rows : rows + 512],
+                os.at[2 * k + n], orr.at[2 * k + n], peer,
+            )
+            copy.start()
+            near.append((copy, ax, full, d, me, peer))
         if d == 1:
             keeps.append(pltpu.make_async_copy(wout.at[:, lo : lo + 256], full.at[me], loads.at[4 + k // 2]))
             keeps[-1].start()
 
-    tree_setup(parents, reach, lags, sinner, sgroup, vinner, vgroup)
-    wst[...] = wstep[...].astype(F32).T.astype(BF16)
-
-    @pl.when(moved)
-    def _():
-        turn.wait()
-
-    @pl.when(jnp.logical_not(moved))
-    def _():
-        keep_tok.wait()
-
     def block(dz):
-        return 2 * ((z + dz) % 8) + c
-
-    cores, ring = [], []
+        return 2 * ((z + dz - r // 2) % 8) + c
+
+    cores, ring, far = [], {}, []
 
     def to_core(dz):
         k = len(cores)
@@ -360,47 +358,36 @@
         copy.start()
         cores.append(copy)
 
-    def hop(dz, d, lo, n):
-        k = len(ring)
-        ref = tg.at[block(dz), lo : lo + n]
-        copy = remote(ref, ref, zs.at[k], zr.at[k], p.at(dz=d))
-        copy.start()
-        ring.append(copy)
-        return copy
-
-    plus, minus = hop(0, 1, 0, 128), hop(0, -1, 0, 128)
-    to_core(0)
-    for s in range(1, 4):
-        rows = 128 if s < 3 else 64
-        plus.wait_recv()
-        plus = hop(-s, 1, 0, rows)
-        minus.wait_recv()
-        minus = hop(s, -1, 128 - rows, rows)
+    def hop(d, s, i):
+        k = (d > 0) * 16 + s * 4 + i
+        ref = tg.at[block(-s * d), 32 * i : 32 * i + 32]
+        ring[d, s, i] = remote(ref, ref, zs.at[k], zr.at[k], p.at(dz=d))
+        ring[d, s, i].start()
+
+    for s in range(4):
+        for i in range(4):
+            for d in (1, -1):
+                if s > 0:
+                    ring[d, s - 1, i].wait_recv()
+                if s < 3 or (d == 1) == (i < 2):
+                    hop(d, s, i)
         to_core(-s)
-        to_core(s)
-    plus.wait_recv()
-    minus.wait_recv()
+        if s > 0:
+            to_core(s)
+        if s == 2:
+            for k, (copy, ax, full, d, me, peer) in enumerate(near[0::2]):
+                copy.wait_recv()
+                lo = 0 if d == 1 else 512
+                ref = full.at[(me - d) % 4, lo : lo + 512]
+                far.append(remote(ref, ref, gs.at[k], gr.at[k], peer))
+                far[-1].start()
+    for i in range(4):
+        ring[1 if i < 2 else -1, 3, i].wait_recv()
     to_core(4)
-    far = []
-    for k, (copy, ax, full, d, me, peer) in enumerate(near):
-        copy.wait_recv()
-        lo = 0 if d == 1 else 512
-        ref = full.at[(me - d) % 4, lo : lo + 512]
-        far.append(remote(ref, ref, gs.at[k], gr.at[k], peer))
-        far[-1].start()
     for copy in cores:
         copy.wait_recv()
     for copy in fetch[:3]:
         copy.wait()
-
-    @pl.loop(0, 16)
-    def _(k):
-        st[k] = dot_nt(wst[...], tg[k])
-
-    @pl.loop(1, 16)
-    def _(j):
-        to = (r + j) % 16
-        remote(st.at[to], sr.at[j], ss, sr_sem, (to, h)).start()
 
     sources = {"group": wgroup, "inner": winner, "gate": wgate}
     results = {"group": vgroup, "inner": vinner, "gate": gate}
@@ -414,83 +401,109 @@
         units.append(pair)
     swap = remote(values.at[c], values.at[c], bc_s, bc_r, p.at(dc=1))
     tail = sr.at[1:16]
+    spread = []
+
+    def part_of_norm(k):
+        at = slice(256 * k, 256 * k + 256)
+        gated = outs_f[:, at] * silu(gate[:, at].astype(F32))
+        norm[k] = (gated * norm_gain[0:1, at]).astype(BF16)
+        for d in (1, 3, 2):
+            for full, peer in ((ny.at[y, k], p.at(dy=d)), (nx.at[x, k], p.at(dx=d))):
+                n = len(spread)
+                copy = remote(norm.at[k], full, ns.at[n], nr.at[n], peer)
+                copy.start()
+                spread.append(copy)
+        nx[x, k] = norm[k]
+        ny[y, k] = norm[k]
+        return gated[:, 0:128] * gated[:, 0:128] + gated[:, 128:256] * gated[:, 128:256]
+
+    squares = jnp.zeros((128, 128), F32)
     for stage, unit in ORDER:
         for one in units[unit]:
             getattr(one, "stage%d" % stage)()
+        if (stage, unit) == (3, 0):
+            @pl.loop(0, 4)
+            def _(k):
+                rows = jnp.concatenate([tg[4 * k + b] for b in range(4)], axis=0)
+                raw = dot_nt(rows, wst[...])
+                for b in range(4):
+                    st[4 * k + b] = raw[128 * b : 128 * b + 128].T
+
+            @pl.loop(1, 16)
+            def _(j):
+                to = (r + j) % 16
+                remote(st.at[to], sr.at[j], ss, sr_sem, (to, h)).start()
+
+        if stage == 5 and unit in (3, 4):
+            for one in units[unit]:
+                squares = squares + part_of_norm(one.column // 256)
         if (stage, unit) == (5, 0):
-            values[c] = tree_conv(vgroup, lags, tgroup, params[2:3, 0:256], 0, 256)
+            values[c] = tree_conv(vgroup, lags, tgroup, biases[0:1, 1024:1280], 0, 256)
             swap.start()
             pltpu.make_async_copy(tail, tail, sr_sem).wait()
             sums = st[r]
             for j in range(1, 16):
                 sums = sums + sr[j]
-            tree_steps(sums, params, reach, path, plen, sizes, cum_t, cum, leaf_w, leaf_e)
+            tree_steps(sums, step_bias, decay_rate, reach, path, plen, sizes, cum_t, cum, leaf_w, leaf_e)
         if stage == 5 and unit in (1, 2):
             for one in units[unit]:
                 lo = one.column
                 channels[:, lo : lo + 256] = tree_conv(
-                    vinner, lags, tinner, params[1:2, lo : lo + 256], lo, 256
+                    vinner, lags, tinner, biases[0:1, lo : lo + 256], lo, 256
                 )
         if (stage, unit) == (5, 2):
             swap.wait_recv()
             fetch[3].wait()
-            tree_outputs(values, states, channels, sizes, cum_t, cum, reach, params, tsize, outs_f)
-
-    squares = jnp.zeros((128, 128), F32)
-    for k in range(8):
-        at = slice(128 * k, 128 * k + 128)
-        gated = outs_f[:, at] * silu(gate[:, at].astype(F32))
-        outs_f[:, at] = gated
-        squares = squares + gated * gated
-    sq_s[...] = squares
+            tree_outputs(values, states, channels, sizes, cum_t, cum, reach, skip_gain, tsize, outs_f)
+
+    sq_s[...] = jnp.broadcast_to(jnp.sum(squares.T, axis=0, keepdims=True), (8, 128))
     trade = remote(sq_s, sq_r, sq_ss, sq_rs, p.at(dc=1))
     trade.start()
     trade.wait_recv()
-    mean = jnp.sum(sq_s[...] + sq_r[...], axis=1, keepdims=True) / GROUP_WIDTH
-    norm[...] = (outs_f[...] * lax.rsqrt(mean + 1e-05) * params[0:1]).astype(BF16)
-
-    spread = []
+    inv[...] = lax.rsqrt((sq_s[...] + sq_r[...]) / GROUP_WIDTH + 1e-05)
+    rates = []
     for d in (1, 3, 2):
-        for full, peer in ((ny.at[y], p.at(dy=d)), (nx.at[x], p.at(dx=d))):
-            k = len(spread)
-            copy = remote(norm, full, ns.at[k], nr.at[k], peer)
+        for full, peer in ((inv_y.at[y], p.at(dy=d)), (inv_x.at[x], p.at(dx=d))):
+            n = len(rates)
+            copy = remote(inv, full, is_.at[n], ir.at[n], peer)
             copy.start()
-            spread.append(copy)
-    nx[x] = norm[...]
-    ny[y] = norm[...]
+            rates.append(copy)
+    inv_x[x] = inv[...]
+    inv_y[y] = inv[...]
     for copy in keeps:
         copy.wait()
-    for copy in far:
+    for copy in far + [one[0] for one in near[1::2]] + spread + rates:
         copy.wait_recv()
 
-    def shard(zz, cc):
-        s = 2 * zz + cc
+    def shard(dz, cc, half):
+        s = 2 * ((z + dz) % 8) + cc
         i, j = s // 4, s % 4
-        return dot(ny[i], wx[j]), dot(nx[j], wy[i])
-
-    for copy in spread:
-        copy.wait_recv()
-
-    @pl.loop(0, 8)
-    def _(zz):
-        left, right = shard(zz, 1 - c)
-        sent[zz, 0] = left.astype(BF16)
-        sent[zz, 1] = right.astype(BF16)
-
-    pass_on = remote(sent, got, ks, kr, p.at(dc=1))
-    pass_on.start()
-
-    @pl.loop(0, 8)
-    def _(zz):
-        left, right = shard(zz, c)
-        own[zz, 0] = left
-        own[zz, 1] = right
-
-    pass_on.wait_recv()
-
-    def mine(dz, half):
-        zz = (z + dz) % 8
-        return own[zz, half] + got[zz, half].astype(F32)
+        rows, scale, weight = ((ny, inv_y, wx), (nx, inv_x, wy))[half]
+        a, b = (i, j) if half == 0 else (j, i)
+        total = dot(rows[a, 0], weight[b, 0:256])
+        for k in range(1, 4):
+            total = total + dot(rows[a, k], weight[b, 256 * k : 256 * k + 256])
+        return total * scale[a].T[:, 0:1]
+
+    passed = {}
+
+    def give(dz):
+        k = dz % 8
+        for half in (0, 1):
+            sent[k, half] = shard(dz, 1 - c, half).astype(BF16)
+        passed[k] = remote(sent.at[k], got.at[k], ks.at[k], kr.at[k], p.at(dc=1))
+        passed[k].start()
+
+    def keep(dz):
+        k = dz % 8
+        for half in (0, 1):
+            own[k, half] = shard(dz, c, half)
+
+    def add(dz):
+        k = dz % 8
+        passed[k].wait_recv()
+        for half in (0, 1):
+            own[k, half] = own[k, half] + got[k, half].astype(F32)
 
     moves = []
 
@@ -511,36 +524,67 @@
         copy.start()
         stores.append(copy)
 
-    zsend_p[0, 0] = mine(4, 0).astype(BF16)
-    plus = move(zsend_p.at[0, 0], zgot_p.at[0, 0], 1)
-    zsend_m[0, 1] = mine(4, 1).astype(BF16)
-    minus = move(zsend_m.at[0, 1], zgot_m.at[0, 1], -1)
-    for s in (1, 2, 3):
-        grow(s - 1)
-        plus.wait_recv()
-        zsend_p[s, 0] = (mine(4 - s, 0) + zgot_p[s - 1, 0].astype(F32)).astype(BF16)
-        if s == 1:
-            zsend_p[s, 1] = mine(4 - s, 1).astype(BF16)
-        else:
-            zsend_p[s, 1] = (mine(4 - s, 1) + zgot_p[s - 1, 1].astype(F32)).astype(BF16)
-        plus = move(zsend_p.at[s], zgot_p.at[s], 1)
-        minus.wait_recv()
-        if s == 1:
-            zsend_m[s, 0] = mine(s - 4, 0).astype(BF16)
-        else:
-            zsend_m[s, 0] = (mine(s - 4, 0) + zgot_m[s - 1, 0].astype(F32)).astype(BF16)
-        zsend_m[s, 1] = (mine(s - 4, 1) + zgot_m[s - 1, 1].astype(F32)).astype(BF16)
-        minus = move(zsend_m.at[s], zgot_m.at[s], -1)
-    grow(3)
-    plus.wait_recv()
-    minus.wait_recv()
+    sends, gots = {1: zsend_p, -1: zsend_m}, {1: zgot_p, -1: zgot_m}
+    chain = {}
+
+    def step(d, s, half, fresh):
+        k = (d * (4 - s)) % 8
+        total = own[k, half]
+        if not fresh:
+            chain[d, half].wait_recv()
+            total = total + gots[d][s - 1, half].astype(F32)
+        sends[d][s, half] = total.astype(BF16)
+        chain[d, half] = move(sends[d].at[s, half], gots[d].at[s, half], d)
+
+    give(4)
+    give(3)
+    give(-3)
+    keep(4)
+    keep(3)
+    keep(-3)
+    add(4)
+    step(1, 0, 0, True)
+    step(-1, 0, 1, True)
+    add(3)
+    step(1, 1, 1, True)
+    add(-3)
+    step(-1, 1, 0, True)
+    give(2)
+    give(-2)
+    keep(2)
+    keep(-2)
+    step(1, 1, 0, False)
+    step(-1, 1, 1, False)
+    add(2)
+    add(-2)
+    step(1, 2, 1, False)
+    step(-1, 2, 0, False)
+    give(1)
+    give(-1)
+    give(0)
+    keep(1)
+    keep(-1)
+    step(1, 2, 0, False)
+    step(-1, 2, 1, False)
+    add(1)
+    add(-1)
+    step(1, 3, 1, False)
+    step(-1, 3, 0, False)
+    keep(0)
+    grow(0)
+    step(1, 3, 0, False)
+    step(-1, 3, 1, False)
+    add(0)
+    grow(1)
 
     def home(half):
         return remote(fin.at[half], land.at[half], fs.at[half], fr.at[half], goal[half])
 
     for half in (0, 1):
+        chain[1, half].wait_recv()
+        chain[-1, half].wait_recv()
         fin[half] = (
-            mine(0, half) + zgot_p[3, half].astype(F32) + zgot_m[3, half].astype(F32)
+            own[0, half] + zgot_p[3, half].astype(F32) + zgot_m[3, half].astype(F32)
         ).astype(BF16)
 
         @pl.when(away[half])
@@ -551,11 +595,15 @@
         def _():
             land[half] = fin[half]
 
+    grow(2)
+    grow(3)
     for pair in units:
         for one in pair:
             one.finish()
     pltpu.make_async_copy(tail, tail, ss).wait()
-    for copy in cores + ring + [one[0] for one in near] + far + [swap, trade, pass_on] + spread + moves:
+    for copy in cores + list(ring.values()) + [one[0] for one in near] + far + [swap, trade]:
+        copy.wait_send()
+    for copy in spread + rates + list(passed.values()) + moves:
         copy.wait_send()
     for copy in stores:
         copy.wait()
@@ -581,22 +629,22 @@
         return pltpu.VMEM(shape, BF16)
 
     scratch = [
-        half(16, 128, 512), flat(16, 16, 128), flat(16, 16, 128), half(16, 512),
+        half(16, 128, 512), flat(16, 16, 128), flat(16, 16, 128),
         half(512, 1024), half(512, 1024), half(512, 256), flat(2, 1024, 256),
         half(4, 1024, 256), half(4, 1024, 256),
         flat(128, 128), half(384, 256), half(256, 1024), half(256, 256), half(128, 1024),
         flat(2, 128, 256), flat(128, 1024), flat(16, 128), flat(16, 128), flat(128, 16),
-        flat(128, 16), flat(16, 256), flat(128, 1024), flat(128, 128), flat(128, 128),
-        half(128, 1024),
-        half(4, 128, 1024), half(4, 128, 1024), flat(8, 2, 128, 256),
+        flat(128, 16), flat(16, 256), flat(128, 1024), flat(8, 128), flat(8, 128),
+        flat(8, 128), flat(4, 8, 128), flat(4, 8, 128), half(4, 128, 256),
+        half(4, 4, 128, 256), half(4, 4, 128, 256), flat(8, 2, 128, 256),
         half(8, 2, 128, 256), half(8, 2, 128, 256),
         half(4, 2, 128, 256), half(4, 2, 128, 256), half(4, 2, 128, 256), half(4, 2, 128, 256),
         half(2, 128, 256), half(2, 128, 256),
-        dma((6,)), dma, dma, dma, dma((8,)), dma((8,)), dma((8,)), dma((8,)), dma, dma,
-        dma((4,)), dma((4,)), dma((4,)), dma((4,)),
+        dma((6,)), dma, dma, dma, dma((32,)), dma((32,)), dma((8,)), dma((8,)), dma, dma,
+        dma((8,)), dma((8,)), dma((4,)), dma((4,)),
         dma((2 * len(UNITS), 8)), dma((2 * len(UNITS), 8)),
-        dma, dma, dma, dma, dma((6,)), dma((6,)), dma, dma, dma((8,)), dma((8,)),
-        dma((2,)), dma((2,)), dma((4,)),
+        dma, dma, dma, dma, dma((6,)), dma((6,)), dma((24,)), dma((24,)), dma((8,)), dma((8,)),
+        dma((14,)), dma((14,)), dma((2,)), dma((2,)), dma((4,)),
     ]
     for _, _, _, width in UNITS:
         scratch += unit_scratch(width) * 2
@@ -605,7 +653,7 @@
         mixer_kernel,
         name="mixer",
         out_shape=(shape((128, 512), BF16), shape((2, 1024, 256), F32)),
-        in_specs=[vmem, hbm, vmem, vmem, hbm, hbm, hbm, vmem, vmem, vmem, vmem, hbm, vmem, vmem, smem, smem],
+        in_specs=[vmem, hbm, vmem, vmem, hbm, hbm, hbm] + [vmem] * 8 + [hbm, vmem, vmem, smem, smem],
         out_specs=(vmem, hbm),
         scratch_shapes=scratch,
         compiler_params=pltpu.CompilerParams(
@@ -620,12 +668,18 @@
     conv_group_bias, step_bias, decay_rate, skip_gain, norm_gain, out_weight, parents,
     accepted_path, path_length, tree_size,
 ):
-    rows = (norm_gain, conv_inner_bias, conv_group_bias, step_bias, decay_rate, skip_gain)
-    params = jnp.stack([jnp.pad(row.astype(F32), (0, 1024 - row.shape[0])) for row in rows])
+    def row(vector):
+        return vector.reshape(1, -1)
+
     mixed, state = mixer(
-        tokens, prior_state.reshape(2, 1024, 256), conv_inner_state, conv_group_state,
-        gate_weight, inner_weight, group_weight, step_weight, conv_inner_weight,
-        conv_group_weight, params, out_weight, parents, accepted_path, path_length, tree_size,
+        tokens, prior_state.reshape(2, 1024, 256), conv_inner_state.swapaxes(0, 1),
+        conv_group_state.swapaxes(0, 1), gate_weight, inner_weight, group_weight, step_weight.T,
+        conv_inner_weight, conv_group_weight,
+        row(lax.optimization_barrier(
+            jnp.concatenate((conv_inner_bias.astype(F32), conv_group_bias.astype(F32)))
+        )),
+        row(step_bias), row(decay_rate), row(skip_gain), row(norm_gain), out_weight, parents,
+        accepted_path, path_length, tree_size,
     )
     return mixed, state.reshape(prior_state.shape)
 

time: 167 us -> 141 us (0.84); the launches traced: 165 us -> 141 us
  Pallas kernels: 151 us -> 134 us
  local copies, waits for them, and re-layouts: 12.1 us -> 5.29 us
    pallas_call x1, Pallas kernels: 151 us -> 134 us  [mixer(): pl.pallas_call(mixer_kernel, name='mixer', out_shape=(shape((128, 512), B...]
    unnamed x5 -> x2, local copies, waits for them, and re-layouts: 8.76 us -> 4.7 us
    pad x3 -> x0, local copies, waits for them, and re-layouts: 1.97 us -> none  [on_device(): jnp.pad(row.astype(F32), (0, 1024 - row.shape[0]))]
where the time goes in v3:
time: 141 us
  Pallas kernels  134 us (95%)
  local copies, waits for them, and re-layouts  5.29 us (4%)
    pallas_call x1, Pallas kernels, mixer(): pl.pallas_call(mixer_kernel, name='mixer', out_shape=(shape((128, 512), B...  134 us
    unnamed x2, local copies, waits for them, and re-layouts  4.7 us

profile of v3, /device:TPU:16, one launch (start us, length us, event | category | flops | bytes accessed | tf_op | source)
XLA Modules:
  0.0 141.0 jit_solution(8460966311127223788)
XLA Ops:
  0.6 0.7 maximum_convert_fusion
  1.3 0.6 reshape.26.refs_10_
  1.9 134.4 %mixer.1 = (bf16[128,512]{1,0:T(8,128)(2,1)}, f32[2,1024,256]{2,1,0:T(8,128)}) custom-call(bf16[128,512]{1,0:T(8,128)(2,1)} %refs_0_.1, f32[2,1024,256]{2,1,0:T(8,128)} %bitcast.9, bf16[3,2,1024]{2,1,0:T(2,128)(2,1)} %bitcast.12, bf16[3,2,256]{2,1,0:T(2,128)(2,1)} %bitcast.14, bf16[512,1024]{1,0:T(8,128)(2,1)} %refs_4_.1, bf16[512,1024]{1,0:T(8,128)(2,1)} %refs_5_.1, ...), custom_call_target="tpu_custom_call" | custom-call | tf_op jit(solution)/shard_map/mixer/pallas_call | solution.py:652
  136.3 1.6 %copy.25 = bf16[128,512]{1,0:T(8,128)(2,1)} copy(bf16[128,512]{1,0:T(8,128)(2,1)} %get-tuple-element.8) | data formatting | bytes 262144
  137.9 3.1 %copy.26 = f32[2,16,64,256]{3,2,1,0:T(8,128)} copy(f32[2,16,64,256]{3,2,1,0:T(8,128)} %bitcast.10) | data formatting | bytes 4194304

commit v4 on v3

--- a/solution.py
+++ b/solution.py
@@ -77,74 +77,93 @@
     return lax.broadcasted_iota(jnp.int32, shape, axis)
 
 
+class Gather:
+    def __init__(self, place, axis, block, full, rows, sems):
+        self.p, self.axis, self.block, self.full, self.rows = place, axis, block, full, rows
+        self.me = place.x if axis == "x" else place.y
+        self.near_s, self.near_r, self.far_s, self.far_r, self.own = sems
+        self.near, self.far = [], []
+
+    def peer(self, d):
+        return self.p.at(dx=d) if self.axis == "x" else self.p.at(dy=d)
+
+    def halves(self, d):
+        half = self.rows // 2
+        first = 0 if d == 1 else half
+        return pl.ds(first, half), pl.ds(half - first, half)
+
+    def start(self):
+        for n in range(2):
+            for i, d in enumerate((1, -1)):
+                rows, k = self.halves(d)[n], 2 * n + i
+                self.near.append(remote(
+                    self.block.at[rows], self.full.at[self.me, rows],
+                    self.near_s.at[k], self.near_r.at[k], self.peer(d),
+                ))
+                self.near[-1].start()
+        self.keep = pltpu.make_async_copy(self.block, self.full.at[self.me], self.own)
+        self.keep.start()
+
+    def forward(self):
+        for i, d in enumerate((1, -1)):
+            self.near[i].wait_recv()
+            ref = self.full.at[(self.me - d) % 4, self.halves(d)[0]]
+            self.far.append(remote(ref, ref, self.far_s.at[i], self.far_r.at[i], self.peer(d)))
+            self.far[-1].start()
+
+    def ready(self):
+        self.keep.wait()
+        for copy in self.near[2:] + self.far:
+            copy.wait_recv()
+
+    def finish(self):
+        for copy in self.near + self.far:
+            copy.wait_send()
+
+
 class Unit:
-    def __init__(self, place, first, weight, column, width, tokens, out, bufs, send, recv):
-        self.p, self.first = place, first
-        self.a, self.b = (place.x, place.y) if first == "x" else (place.y, place.x)
-        self.weight, self.column, self.width = weight, column, width
+    def __init__(self, place, along, gather, column, width, tokens, out, bufs, send, recv):
+        self.p, self.along = place, along
+        self.b = place.y if along == "y" else place.x
+        self.gather, self.column, self.width = gather, column, width
         self.tokens, self.out = tokens, out
-        (self.s1, self.rf, self.s2p, self.s2m, self.rgp, self.rgm, self.q,
-         self.s3, self.rh, self.s4p, self.s4m, self.rip, self.rim) = bufs
+        self.q, self.s3, self.rh, self.s4p, self.s4m, self.rip, self.rim = bufs
         self.send, self.recv = send, recv
         self.copies = {}
 
-    def along(self, which, step):
-        name = self.first if which == "a" else ("y" if self.first == "x" else "x")
-        return self.p.at(dy=step) if name == "y" else self.p.at(dx=step)
-
-    def part(self, dest_a):
-        slots = [4 * b + dest_a if self.first == "x" else 4 * dest_a + b for b in range(4)]
-        rows = jnp.concatenate([self.tokens[slot] for slot in slots], axis=0)
-        return dot(rows, self.weight[:, self.column : self.column + self.width])
-
-    def put(self, k, src, dst, which, step):
-        copy = remote(src, dst, self.send.at[k], self.recv.at[k], self.along(which, step))
+    def put(self, k, src, dst, step):
+        peer = self.p.at(dy=step) if self.along == "y" else self.p.at(dx=step)
+        copy = remote(src, dst, self.send.at[k], self.recv.at[k], peer)
         copy.start()
         self.copies[k] = copy
 
     def stage1(self):
-        far = self.part((self.a + 2) % 4).astype(BF16)
+        self.gather.ready()
+        total = None
+        for k in range(4):
+            rows = jnp.concatenate([self.tokens[b, k] for b in range(4)], axis=0)
+            term = dot(rows, self.gather.full[k])
+            total = term if total is None else total + term
         for b in range(4):
-            self.s1[b] = far[128 * b : 128 * b + 128]
-        self.put(0, self.s1.at[0:2], self.rf.at[0:2], "a", 1)
-        self.put(1, self.s1.at[2:4], self.rf.at[2:4], "a", -1)
+            self.q[b] = total[128 * b : 128 * b + 128]
+        self.s3[...] = self.q[(self.b + 2) % 4].astype(BF16)
+        self.put(0, self.s3.at[0:64], self.rh.at[0:64], 1)
+        self.put(1, self.s3.at[64:128], self.rh.at[64:128], -1)
 
     def stage2(self):
-        for k, step, to, whole in ((0, 1, self.s2p, self.rgp), (1, -1, self.s2m, self.rgm)):
-            terms = self.part((self.a + step) % 4)
-            self.copies[k].wait_recv()
-            for b in range(4):
-                term = terms[128 * b : 128 * b + 128]
-                if b // 2 == k:
-                    term = term + self.rf[b].astype(F32)
-                to[b] = term.astype(BF16)
-            self.put(2 + k, to, whole, "a", step)
-
-    def stage3(self):
-        terms = self.part(self.a)
-        self.copies[2].wait_recv()
-        self.copies[3].wait_recv()
-        for b in range(4):
-            term = terms[128 * b : 128 * b + 128]
-            self.q[b] = term + self.rgp[b].astype(F32) + self.rgm[b].astype(F32)
-        self.s3[...] = self.q[(self.b + 2) % 4].astype(BF16)
-        self.put(4, self.s3.at[0:64], self.rh.at[0:64], "b", 1)
-        self.put(5, self.s3.at[64:128], self.rh.at[64:128], "b", -1)
-
-    def stage4(self):
-        self.copies[4].wait_recv()
-        self.copies[5].wait_recv()
+        self.copies[0].wait_recv()
+        self.copies[1].wait_recv()
         up, down = (self.b + 1) % 4, (self.b + 3) % 4
         self.s4p[0:64] = (self.q[up, 0:64] + self.rh[0:64].astype(F32)).astype(BF16)
         self.s4p[64:128] = self.q[up, 64:128].astype(BF16)
         self.s4m[0:64] = self.q[down, 0:64].astype(BF16)
         self.s4m[64:128] = (self.q[down, 64:128] + self.rh[64:128].astype(F32)).astype(BF16)
-        self.put(6, self.s4p, self.rip, "b", 1)
-        self.put(7, self.s4m, self.rim, "b", -1)
-
-    def stage5(self):
-        self.copies[6].wait_recv()
-        self.copies[7].wait_recv()
+        self.put(2, self.s4p, self.rip, 1)
+        self.put(3, self.s4m, self.rim, -1)
+
+    def stage3(self):
+        self.copies[2].wait_recv()
+        self.copies[3].wait_recv()
         total = self.q[self.b] + self.rip[...].astype(F32) + self.rim[...].astype(F32)
         self.out[0:128, self.column : self.column + self.width] = total.astype(BF16)
 
@@ -154,11 +173,8 @@
 
 
 def unit_scratch(width):
-    def block(n, dtype=BF16):
-        return pltpu.VMEM((n, 128, width), dtype)
-
     flat = pltpu.VMEM((128, width), BF16)
-    return [block(4)] * 6 + [block(4, F32)] + [flat] * 6
+    return [pltpu.VMEM((4, 128, width), F32)] + [flat] * 6
 
 
 def tree_setup(parents, reach, lags, priors):
@@ -271,9 +287,8 @@
 
 
 ORDER = (
-    (1, 0), (1, 1), (2, 0), (1, 2), (2, 1), (3, 0), (1, 3), (2, 2), (3, 1), (4, 0), (1, 4),
-    (3, 2), (4, 1), (5, 0), (2, 3), (4, 2), (5, 1), (2, 4), (5, 2),
-    (3, 3), (3, 4), (4, 3), (4, 4), (5, 3), (5, 4),
+    (1, 0), (1, 1), (1, 2), (2, 0), (1, 3), (2, 1), (3, 0), (1, 4), (2, 2), (3, 1),
+    (2, 3), (3, 2), (2, 4), (3, 3), (3, 4),
 )
 
 
@@ -281,126 +296,158 @@
     (tok, state, sinner, sgroup, wgate_hbm, winner_hbm, wgroup_hbm, wst, tinner, tgroup,
      biases, step_bias, decay_rate, skip_gain, norm_gain, wout, parents, path, plen, tsize,
      mixed, next_state,
-     tg, st, sr, wgate, winner, wgroup, states, wx, wy,
+     tx, ty, wsg, st, sr, states, wx, wy,
      reach, lags, vinner, vgroup, gate, values, channels, sizes, cum_t, cum, leaf_w, leaf_e,
      outs_f, sq_s, sq_r, inv, inv_x, inv_y, norm,
      nx, ny, own, sent, got, zsend_p, zsend_m, zgot_p, zgot_m, fin, land,
-     loads, turn_s, turn_r, local, zs, zr, cs, cr, ss, sr_sem, os, orr, gs, gr, us, ur,
-     bc_s, bc_r, sq_ss, sq_rs, is_, ir, ns, nr, ks, kr, vs, vr, fs, fr, store) = refs[:92]
-    bufs = refs[92:]
+     loads, turn_s, turn_r, zs, zr, cs, cr, ws_s, ws_r, ss, sr_sem, near_s, near_r, far_s, far_r, own_sem, us, ur,
+     bc_s, bc_r, sq_ss, sq_rs, is_, ir, ns, nr, ks, kr, vs, vr, fs, fr, store) = refs[:93]
+    bufs = refs[93:]
     p = Place()
     r, h, y, x, z, c = p.r, p.h, p.y, p.x, p.z, p.c
     hy, hx = h // 4, h % 4
-    turn_to = (h, 2 * ((z + r // 2) % 8) + r % 2)
-    turn_from = (2 * ((z - r // 2) % 8) + c, r)
-    moved = jnp.logical_or(turn_to[0] != r, turn_to[1] != h)
+    turns = (
+        (tx, (z // 2 * 4 + x, 2 * ((z + 2 * y) % 8) + c),
+         ((z // 2 - y) % 4 * 4 + x, 2 * (2 * y + z % 2) + c)),
+        (ty, (y * 4 + 2 * (z % 2) + c, 2 * ((z + x // 2) % 8) + x % 2),
+         (y * 4 + 2 * ((z - x // 2) % 2) + c, 2 * ((z - (z - x // 2) % 2) % 8) + x % 2)),
+    )
+    moved = [jnp.logical_or(to[0] != r, to[1] != h) for _, to, _ in turns]
     goal = ((hy * 4 + x, y * 4 + hx), (y * 4 + hx, hy * 4 + x))
     away = (hy != y, hx != x)
 
-    fetch = []
-    for k, (src, dst) in enumerate(
-        ((wgroup_hbm, wgroup), (winner_hbm, winner), (wgate_hbm, wgate), (state, states))
-    ):
-        fetch.append(pltpu.make_async_copy(src, dst, loads.at[k]))
-        fetch[-1].start()
+    fetch = pltpu.make_async_copy(state, states, loads)
+    fetch.start()
+
+    sources = {"group": wgroup_hbm, "inner": winner_hbm, "gate": wgate_hbm}
+    results = {"group": vgroup, "inner": vinner, "gate": gate}
+    gathers, units = [], []
+    for i, (name, xcol, ycol, width) in enumerate(UNITS):
+        pair = []
+        for j, (axis, col) in enumerate((("x", xcol), ("y", ycol))):
+            n = 2 * i + j
+            gathers.append(Gather(
+                p, axis, sources[name].at[:, col : col + width], bufs[8 * n], 512,
+                (near_s.at[n], near_r.at[n], far_s.at[n], far_r.at[n], own_sem.at[n]),
+            ))
+            pair.append(Unit(p, "y" if axis == "x" else "x", gathers[-1], col, width, (tx, ty)[j],
+                             results[name], bufs[8 * n + 1 : 8 * n + 8], us.at[n], ur.at[n]))
+        units.append(pair)
+    for j, (axis, full) in enumerate((("x", wx), ("y", wy))):
+        n = 2 * len(UNITS) + j
+        gathers.append(Gather(
+            p, axis, wout.at[:, 256 * j : 256 * j + 256], full, 1024,
+            (near_s.at[n], near_r.at[n], far_s.at[n], far_r.at[n], own_sem.at[n]),
+        ))
+
+    def start(i):
+        for one in gathers[2 * i : 2 * i + 2]:
+            one.start()
+
+    def forward(i):
+        for one in gathers[2 * i : 2 * i + 2]:
+            one.forward()
 
     meet(
-        [((r + j) % 16, h) for j in range(1, 16)] + [p.at(dz=1), p.at(dz=-1), p.at(dc=1)],
-        [(turn_from, moved), (goal[0], away[0]), (goal[1], away[1])],
+        [p.at(dy=d) for d in (1, 2, 3)] + [p.at(dx=d) for d in (1, 2, 3)]
+        + [p.at(dz=1), p.at(dz=-1), p.at(dc=1)],
+        [(turns[0][2], moved[0]), (turns[1][2], moved[1]), (goal[0], away[0]), (goal[1], away[1])],
     )
-    turn = remote(tok, tg.at[r], turn_s, turn_r, turn_to)
-    keep_tok = pltpu.make_async_copy(tok, tg.at[r], local)
-
-    @pl.when(moved)
-    def _():
-        turn.start()
-
-    @pl.when(jnp.logical_not(moved))
-    def _():
-        keep_tok.start()
+
+    def place_x(dz):
+        zz = (z + dz) % 8
+        return (zz // 2 - y) % 4, 2 * (zz % 2) + c
+
+    def place_y(dz):
+        zz = (z + dz) % 8
+        high = (zz - x // 2) % 2
+        return 2 * high + c, (zz - high) % 8 // 2
+
+    def slot(j, dz):
+        return tx.at[place_x(dz)] if j == 0 else ty.at[place_y(dz)]
+
+    def turn_send(j):
+        full, to, _ = turns[j]
+        there = (y, 2 * (z % 2) + c) if j == 0 else (x, z // 2)
+        return remote(tok, full.at[there], turn_s.at[j], turn_r.at[j], to)
+
+    for j in range(2):
+
+        @pl.when(moved[j])
+        def _():
+            turn_send(j).start()
+
+        @pl.when(jnp.logical_not(moved[j]))
+        def _():
+            pltpu.make_async_copy(tok, slot(j, 0), turn_s.at[j]).start()
+
+    start(0)
+    start(1)
+    start(2)
+    small = []
+    for d in (1, 2, 3):
+        copy = remote(wst, wsg.at[x], ws_s.at[d - 1], ws_r.at[d - 1], p.at(dx=d))
+        copy.start()
+        small.append(copy)
+    wsg[x] = wst[...]
 
     tree_setup(parents, reach, lags, ((sinner, vinner), (sgroup, vgroup)))
 
-    @pl.when(moved)
-    def _():
-        turn.wait()
-
-    @pl.when(jnp.logical_not(moved))
-    def _():
-        keep_tok.wait()
-
-    near, keeps = [], []
-    for k, (ax, full, lo, d) in enumerate(
-        (("x", wx, 0, 1), ("x", wx, 0, -1), ("y", wy, 256, 1), ("y", wy, 256, -1))
-    ):
-        me = x if ax == "x" else y
-        peer = p.at(dx=d) if ax == "x" else p.at(dy=d)
-        first = 0 if d == 1 else 512
-        for n, rows in enumerate((first, 512 - first)):
-            copy = remote(
-                wout.at[rows : rows + 512, lo : lo + 256], full.at[me, rows : rows + 512],
-                os.at[2 * k + n], orr.at[2 * k + n], peer,
-            )
-            copy.start()
-            near.append((copy, ax, full, d, me, peer))
-        if d == 1:
-            keeps.append(pltpu.make_async_copy(wout.at[:, lo : lo + 256], full.at[me], loads.at[4 + k // 2]))
-            keeps[-1].start()
-
-    def block(dz):
-        return 2 * ((z + dz - r // 2) % 8) + c
-
-    cores, ring, far = [], {}, []
-
-    def to_core(dz):
+    for j in range(2):
+
+        @pl.when(moved[j])
+        def _():
+            turn_send(j).wait()
+
+        @pl.when(jnp.logical_not(moved[j]))
+        def _():
+            pltpu.make_async_copy(tok, slot(j, 0), turn_s.at[j]).wait()
+
+    cores, ring = [], {}
+
+    def to_core(j, dz):
         k = len(cores)
-        copy = remote(tg.at[block(dz)], tg.at[block(dz)], cs.at[k], cr.at[k], p.at(dc=1))
+        copy = remote(slot(j, dz), slot(j, dz), cs.at[k], cr.at[k], p.at(dc=1))
         copy.start()
         cores.append(copy)
 
-    def hop(d, s, i):
-        k = (d > 0) * 16 + s * 4 + i
-        ref = tg.at[block(-s * d), 32 * i : 32 * i + 32]
-        ring[d, s, i] = remote(ref, ref, zs.at[k], zr.at[k], p.at(dz=d))
-        ring[d, s, i].start()
+    def hop(d, s, j, i):
+        k = len(ring)
+        ref = slot(j, -s * d).at[64 * i : 64 * i + 64]
+        ring[d, s, j, i] = remote(ref, ref, zs.at[k], zr.at[k], p.at(dz=d))
+        ring[d, s, j, i].start()
 
     for s in range(4):
-        for i in range(4):
-            for d in (1, -1):
-                if s > 0:
-                    ring[d, s - 1, i].wait_recv()
-                if s < 3 or (d == 1) == (i < 2):
-                    hop(d, s, i)
-        to_core(-s)
-        if s > 0:
-            to_core(s)
+        for j in range(2):
+            for i in range(2):
+                for d in (1, -1):
+                    if s > 0:
+                        ring[d, s - 1, j, i].wait_recv()
+                    if s < 3 or (d == 1) == (i == 0):
+                        hop(d, s, j, i)
+            to_core(j, -s)
+            if s > 0:
+                to_core(j, s)
+        if s == 0:
+            forward(0)
+            start(3)
+        if s == 1:
+            forward(1)
+            forward(2)
+            start(4)
         if s == 2:
-            for k, (copy, ax, full, d, me, peer) in enumerate(near[0::2]):
-                copy.wait_recv()
-                lo = 0 if d == 1 else 512
-                ref = full.at[(me - d) % 4, lo : lo + 512]
-                far.append(remote(ref, ref, gs.at[k], gr.at[k], peer))
-                far[-1].start()
-    for i in range(4):
-        ring[1 if i < 2 else -1, 3, i].wait_recv()
-    to_core(4)
+            forward(3)
+        if s == 3:
+            forward(4)
+    for j in range(2):
+        ring[1, 3, j, 0].wait_recv()
+        ring[-1, 3, j, 1].wait_recv()
+        to_core(j, 4)
     for copy in cores:
         copy.wait_recv()
-    for copy in fetch[:3]:
-        copy.wait()
-
-    sources = {"group": wgroup, "inner": winner, "gate": wgate}
-    results = {"group": vgroup, "inner": vinner, "gate": gate}
-    units = []
-    for i, (name, xcol, ycol, width) in enumerate(UNITS):
-        pair = []
-        for j, (first, col) in enumerate((("x", xcol), ("y", ycol))):
-            n = 2 * i + j
-            pair.append(Unit(p, first, sources[name], col, width, tg, results[name],
-                             bufs[13 * n : 13 * n + 13], us.at[n], ur.at[n]))
-        units.append(pair)
+
     swap = remote(values.at[c], values.at[c], bc_s, bc_r, p.at(dc=1))
-    tail = sr.at[1:16]
+    tail = sr.at[1:4]
     spread = []
 
     def part_of_norm(k):
@@ -421,40 +468,42 @@
     for stage, unit in ORDER:
         for one in units[unit]:
             getattr(one, "stage%d" % stage)()
-        if (stage, unit) == (3, 0):
-            @pl.loop(0, 4)
-            def _(k):
-                rows = jnp.concatenate([tg[4 * k + b] for b in range(4)], axis=0)
-                raw = dot_nt(rows, wst[...])
-                for b in range(4):
-                    st[4 * k + b] = raw[128 * b : 128 * b + 128].T
-
-            @pl.loop(1, 16)
-            def _(j):
-                to = (r + j) % 16
-                remote(st.at[to], sr.at[j], ss, sr_sem, (to, h)).start()
-
-        if stage == 5 and unit in (3, 4):
+        if (stage, unit) == (1, 2):
+            for copy in small:
+                copy.wait_recv()
+            raw = None
+            for k in range(4):
+                rows = jnp.concatenate([tx[b, k] for b in range(4)], axis=0)
+                term = dot_nt(rows, wsg[k])
+                raw = term if raw is None else raw + term
+            for b in range(4):
+                st[b] = raw[128 * b : 128 * b + 128].T
+            for d in (1, 2, 3):
+                remote(st.at[(y + d) % 4], sr.at[d], ss, sr_sem, p.at(dy=d)).start()
+
+        if stage == 3 and unit in (3, 4):
             for one in units[unit]:
                 squares = squares + part_of_norm(one.column // 256)
-        if (stage, unit) == (5, 0):
+        if (stage, unit) == (3, 0):
             values[c] = tree_conv(vgroup, lags, tgroup, biases[0:1, 1024:1280], 0, 256)
             swap.start()
             pltpu.make_async_copy(tail, tail, sr_sem).wait()
-            sums = st[r]
-            for j in range(1, 16):
+            sums = st[y]
+            for j in range(1, 4):
                 sums = sums + sr[j]
             tree_steps(sums, step_bias, decay_rate, reach, path, plen, sizes, cum_t, cum, leaf_w, leaf_e)
-        if stage == 5 and unit in (1, 2):
+        if stage == 3 and unit in (1, 2):
             for one in units[unit]:
                 lo = one.column
                 channels[:, lo : lo + 256] = tree_conv(
                     vinner, lags, tinner, biases[0:1, lo : lo + 256], lo, 256
                 )
-        if (stage, unit) == (5, 2):
+        if (stage, unit) == (2, 4):
+            start(5)
             swap.wait_recv()
-            fetch[3].wait()
+            fetch.wait()
             tree_outputs(values, states, channels, sizes, cum_t, cum, reach, skip_gain, tsize, outs_f)
+            forward(5)
 
     sq_s[...] = jnp.broadcast_to(jnp.sum(squares.T, axis=0, keepdims=True), (8, 128))
     trade = remote(sq_s, sq_r, sq_ss, sq_rs, p.at(dc=1))
@@ -470,9 +519,9 @@
             rates.append(copy)
     inv_x[x] = inv[...]
     inv_y[y] = inv[...]
-    for copy in keeps:
-        copy.wait()
-    for copy in far + [one[0] for one in near[1::2]] + spread + rates:
+    for one in gathers[10:12]:
+        one.ready()
+    for copy in spread + rates:
         copy.wait_recv()
 
     def shard(dz, cc, half):
@@ -601,7 +650,9 @@
         for one in pair:
             one.finish()
     pltpu.make_async_copy(tail, tail, ss).wait()
-    for copy in cores + list(ring.values()) + [one[0] for one in near] + far + [swap, trade]:
+    for one in gathers:
+        one.finish()
+    for copy in cores + list(ring.values()) + small + [swap, trade]:
         copy.wait_send()
     for copy in spread + rates + list(passed.values()) + moves:
         copy.wait_send()
@@ -629,8 +680,8 @@
         return pltpu.VMEM(shape, BF16)
 
     scratch = [
-        half(16, 128, 512), flat(16, 16, 128), flat(16, 16, 128),
-        half(512, 1024), half(512, 1024), half(512, 256), flat(2, 1024, 256),
+        half(4, 4, 128, 512), half(4, 4, 128, 512), half(4, 16, 512), flat(4, 16, 128),
+        flat(4, 16, 128), flat(2, 1024, 256),
         half(4, 1024, 256), half(4, 1024, 256),
         flat(128, 128), half(384, 256), half(256, 1024), half(256, 256), half(128, 1024),
         flat(2, 128, 256), flat(128, 1024), flat(16, 128), flat(16, 128), flat(128, 16),
@@ -640,14 +691,14 @@
         half(8, 2, 128, 256), half(8, 2, 128, 256),
         half(4, 2, 128, 256), half(4, 2, 128, 256), half(4, 2, 128, 256), half(4, 2, 128, 256),
         half(2, 128, 256), half(2, 128, 256),
-        dma((6,)), dma, dma, dma, dma((32,)), dma((32,)), dma((8,)), dma((8,)), dma, dma,
-        dma((8,)), dma((8,)), dma((4,)), dma((4,)),
-        dma((2 * len(UNITS), 8)), dma((2 * len(UNITS), 8)),
+        dma, dma((2,)), dma((2,)), dma((28,)), dma((28,)), dma((16,)), dma((16,)), dma((3,)), dma((3,)), dma, dma,
+        dma((12, 4)), dma((12, 4)), dma((12, 2)), dma((12, 2)), dma((12,)),
+        dma((2 * len(UNITS), 4)), dma((2 * len(UNITS), 4)),
         dma, dma, dma, dma, dma((6,)), dma((6,)), dma((24,)), dma((24,)), dma((8,)), dma((8,)),
         dma((14,)), dma((14,)), dma((2,)), dma((2,)), dma((4,)),
     ]
     for _, _, _, width in UNITS:
-        scratch += unit_scratch(width) * 2
+        scratch += ([half(4, 512, width)] + unit_scratch(width)) * 2
     shape = jax.ShapeDtypeStruct
     return pl.pallas_call(
         mixer_kernel,

time: 141 us -> 135 us (0.957)
  Pallas kernels: 134 us -> 128 us
    pallas_call x1, Pallas kernels: 134 us -> 128 us  [mixer(): pl.pallas_call(mixer_kernel, name='mixer', out_shape=(shape((128, 512), B...]
where the time goes in v4:
time: 135 us
  Pallas kernels  128 us (95%)
  local copies, waits for them, and re-layouts  5.29 us (4%)
    pallas_call x1, Pallas kernels, mixer(): pl.pallas_call(mixer_kernel, name='mixer', out_shape=(shape((128, 512), B...  128 us
    unnamed x2, local copies, waits for them, and re-layouts  4.7 us

profile of v4, /device:TPU:16, one launch (start us, length us, event | category | flops | bytes accessed | tf_op | source)
XLA Modules:
  0.0 134.5 jit_solution(9291291664630603032)
XLA Ops:
  0.6 0.7 maximum_convert_fusion
  1.3 0.6 reshape.26.refs_10_
  1.9 127.9 %mixer.1 = (bf16[128,512]{1,0:T(8,128)(2,1)}, f32[2,1024,256]{2,1,0:T(8,128)}) custom-call(bf16[128,512]{1,0:T(8,128)(2,1)} %refs_0_.1, f32[2,1024,256]{2,1,0:T(8,128)} %bitcast.9, bf16[3,2,1024]{2,1,0:T(2,128)(2,1)} %bitcast.12, bf16[3,2,256]{2,1,0:T(2,128)(2,1)} %bitcast.14, bf16[512,1024]{1,0:T(8,128)(2,1)} %refs_4_.1, bf16[512,1024]{1,0:T(8,128)(2,1)} %refs_5_.1, ...), custom_call_target="tpu_custom_call" | custom-call | tf_op jit(solution)/shard_map/mixer/pallas_call | solution.py:703
  129.8 1.6 %copy.25 = bf16[128,512]{1,0:T(8,128)(2,1)} copy(bf16[128,512]{1,0:T(8,128)(2,1)} %get-tuple-element.8) | data formatting | bytes 262144
  131.4 3.1 %copy.26 = f32[2,16,64,256]{3,2,1,0:T(8,128)} copy(f32[2,16,64,256]{3,2,1,0:T(8,128)} %bitcast.10) | data formatting | bytes 4194304

commit v5 on v4

--- a/solution.py
+++ b/solution.py
@@ -92,17 +92,20 @@
         first = 0 if d == 1 else half
         return pl.ds(first, half), pl.ds(half - first, half)
 
+    def load(self):
+        self.keep = pltpu.make_async_copy(self.block, self.full.at[self.me], self.own)
+        self.keep.start()
+
     def start(self):
+        self.keep.wait()
         for n in range(2):
             for i, d in enumerate((1, -1)):
                 rows, k = self.halves(d)[n], 2 * n + i
                 self.near.append(remote(
-                    self.block.at[rows], self.full.at[self.me, rows],
+                    self.full.at[self.me, rows], self.full.at[self.me, rows],
                     self.near_s.at[k], self.near_r.at[k], self.peer(d),
                 ))
                 self.near[-1].start()
-        self.keep = pltpu.make_async_copy(self.block, self.full.at[self.me], self.own)
-        self.keep.start()
 
     def forward(self):
         for i, d in enumerate((1, -1)):
@@ -112,7 +115,6 @@
             self.far[-1].start()
 
     def ready(self):
-        self.keep.wait()
         for copy in self.near[2:] + self.far:
             copy.wait_recv()
 
@@ -241,29 +243,36 @@
     leaf_w[...] = (weights * size).T
 
 
-def tree_outputs(values, states, channels, sizes, cum_t, cum, reach, gain, tsize, out):
+def tree_mixes(values, states, sizes, cum_t, cum, reach, mixes, out):
+    c_half = values[1].astype(BF16)
+    meet_bc = dot_nt(c_half, values[0].astype(BF16))
+    linked = reach[...] > 0
+    for head in range(16):
+        column, across = cum[:, head : head + 1], cum_t[head : head + 1]
+        decay = jnp.where(linked, jnp.exp(jnp.minimum(column - across, 0.0)), 0.0)
+        mixes[head // 2, :, 128 * (head % 2) : 128 * (head % 2) + 128] = (
+            decay * meet_bc * sizes[head : head + 1]
+        ).astype(BF16)
     for q in range(2):
         rows = slice(64 * q, 64 * q + 64)
-        out[rows] = dot_nt(values[1, rows], states[q], TREE_PRECISION)
-    meet_bc = dot_nt(values[1], values[0], TREE_PRECISION)
-    linked = reach[...] > 0
+        out[rows] = dot_nt(c_half[rows], states[q].astype(BF16))
+
+
+def tree_outputs(pairs, channels, cum, mixes, gain, tsize, out):
     lane = iota((128, 128), 1) < 64
     row = iota((128, 1), 0)
     valid = jnp.where(row < 64, row, row - 64) < jnp.where(row < 64, tsize[0], tsize[1])
-    for pair in range(8):
+    for pair in pairs:
         at = slice(128 * pair, 128 * pair + 128)
         x = channels[:, at]
-        mixes, grown, skips = [], [], []
-        for head in (2 * pair, 2 * pair + 1):
-            column, across = cum[:, head : head + 1], cum_t[head : head + 1]
-            decay = jnp.where(linked, jnp.exp(jnp.minimum(column - across, 0.0)), 0.0)
-            mixes.append(decay * meet_bc * sizes[head : head + 1])
-            grown.append(jnp.exp(column))
-            skips.append(gain[0:1, head : head + 1])
+        heads = (2 * pair, 2 * pair + 1)
+        grown = [jnp.exp(cum[:, head : head + 1]) for head in heads]
+        skips = [gain[0:1, head : head + 1] for head in heads]
         both = dot(
-            jnp.concatenate(mixes, axis=1),
-            jnp.concatenate((jnp.where(lane, x, 0.0), jnp.where(lane, 0.0, x)), axis=0),
-            TREE_PRECISION,
+            mixes[pair],
+            jnp.concatenate(
+                (jnp.where(lane, x, 0.0).astype(BF16), jnp.where(lane, 0.0, x).astype(BF16)), axis=0
+            ),
         )
         total = both + jnp.where(lane, grown[0], grown[1]) * out[:, at]
         total = total + jnp.where(lane, skips[0], skips[1]) * x
@@ -287,8 +296,8 @@
 
 
 ORDER = (
-    (1, 0), (1, 1), (1, 2), (2, 0), (1, 3), (2, 1), (3, 0), (1, 4), (2, 2), (3, 1),
-    (2, 3), (3, 2), (2, 4), (3, 3), (3, 4),
+    (1, 0), (1, 1), (2, 0), (1, 2), (3, 0), (2, 1), (1, 3), (2, 2), (1, 4), (2, 3), (3, 1), (2, 4),
+    (3, 2), (3, 3), (3, 4),
 )
 
 
@@ -297,12 +306,12 @@
      biases, step_bias, decay_rate, skip_gain, norm_gain, wout, parents, path, plen, tsize,
      mixed, next_state,
      tx, ty, wsg, st, sr, states, wx, wy,
-     reach, lags, vinner, vgroup, gate, values, channels, sizes, cum_t, cum, leaf_w, leaf_e,
+     reach, lags, vinner, vgroup, gate, values, channels, sizes, cum_t, cum, leaf_w, leaf_e, mixes,
      outs_f, sq_s, sq_r, inv, inv_x, inv_y, norm,
      nx, ny, own, sent, got, zsend_p, zsend_m, zgot_p, zgot_m, fin, land,
      loads, turn_s, turn_r, zs, zr, cs, cr, ws_s, ws_r, ss, sr_sem, near_s, near_r, far_s, far_r, own_sem, us, ur,
-     bc_s, bc_r, sq_ss, sq_rs, is_, ir, ns, nr, ks, kr, vs, vr, fs, fr, store) = refs[:93]
-    bufs = refs[93:]
+     bc_s, bc_r, sq_ss, sq_rs, is_, ir, ns, nr, ks, kr, vs, vr, fs, fr, store) = refs[:94]
+    bufs = refs[94:]
     p = Place()
     r, h, y, x, z, c = p.r, p.h, p.y, p.x, p.z, p.c
     hy, hx = h // 4, h % 4
@@ -317,7 +326,6 @@
     away = (hy != y, hx != x)
 
     fetch = pltpu.make_async_copy(state, states, loads)
-    fetch.start()
 
     sources = {"group": wgroup_hbm, "inner": winner_hbm, "gate": wgate_hbm}
     results = {"group": vgroup, "inner": vinner, "gate": gate}
@@ -348,6 +356,9 @@
         for one in gathers[2 * i : 2 * i + 2]:
             one.forward()
 
+    for one in gathers:
+        one.load()
+    fetch.start()
     meet(
         [p.at(dy=d) for d in (1, 2, 3)] + [p.at(dx=d) for d in (1, 2, 3)]
         + [p.at(dz=1), p.at(dz=-1), p.at(dc=1)],
@@ -384,6 +395,8 @@
     start(0)
     start(1)
     start(2)
+    start(3)
+    start(4)
     small = []
     for d in (1, 2, 3):
         copy = remote(wst, wsg.at[x], ws_s.at[d - 1], ws_r.at[d - 1], p.at(dx=d))
@@ -393,16 +406,6 @@
 
     tree_setup(parents, reach, lags, ((sinner, vinner), (sgroup, vgroup)))
 
-    for j in range(2):
-
-        @pl.when(moved[j])
-        def _():
-            turn_send(j).wait()
-
-        @pl.when(jnp.logical_not(moved[j]))
-        def _():
-            pltpu.make_async_copy(tok, slot(j, 0), turn_s.at[j]).wait()
-
     cores, ring = [], {}
 
     def to_core(j, dz):
@@ -418,7 +421,17 @@
         ring[d, s, j, i].start()
 
     for s in range(4):
-        for j in range(2):
+        for j in (1, 0):
+            if s == 0:
+
+                @pl.when(moved[j])
+                def _():
+                    turn_send(j).wait()
+
+                @pl.when(jnp.logical_not(moved[j]))
+                def _():
+                    pltpu.make_async_copy(tok, slot(j, 0), turn_s.at[j]).wait()
+
             for i in range(2):
                 for d in (1, -1):
                     if s > 0:
@@ -430,16 +443,14 @@
                 to_core(j, s)
         if s == 0:
             forward(0)
-            start(3)
         if s == 1:
             forward(1)
             forward(2)
-            start(4)
         if s == 2:
             forward(3)
-        if s == 3:
-            forward(4)
-    for j in range(2):
+    forward(4)
+    start(5)
+    for j in (1, 0):
         ring[1, 3, j, 0].wait_recv()
         ring[-1, 3, j, 1].wait_recv()
         to_core(j, 4)
@@ -468,7 +479,7 @@
     for stage, unit in ORDER:
         for one in units[unit]:
             getattr(one, "stage%d" % stage)()
-        if (stage, unit) == (1, 2):
+        if (stage, unit) == (1, 1):
             for copy in small:
                 copy.wait_recv()
             raw = None
@@ -498,11 +509,15 @@
                 channels[:, lo : lo + 256] = tree_conv(
                     vinner, lags, tinner, biases[0:1, lo : lo + 256], lo, 256
                 )
-        if (stage, unit) == (2, 4):
-            start(5)
+        if (stage, unit) == (1, 4):
             swap.wait_recv()
             fetch.wait()
-            tree_outputs(values, states, channels, sizes, cum_t, cum, reach, skip_gain, tsize, outs_f)
+            tree_mixes(values, states, sizes, cum_t, cum, reach, mixes, outs_f)
+        if stage == 3 and unit in (1, 2):
+            for one in units[unit]:
+                lo = one.column // 128
+                tree_outputs((lo, lo + 1), channels, cum, mixes, skip_gain, tsize, outs_f)
+        if (stage, unit) == (3, 0):
             forward(5)
 
     sq_s[...] = jnp.broadcast_to(jnp.sum(squares.T, axis=0, keepdims=True), (8, 128))
@@ -586,14 +601,14 @@
         chain[d, half] = move(sends[d].at[s, half], gots[d].at[s, half], d)
 
     give(4)
+    keep(4)
     give(3)
-    give(-3)
-    keep(4)
-    keep(3)
-    keep(-3)
     add(4)
     step(1, 0, 0, True)
     step(-1, 0, 1, True)
+    keep(3)
+    give(-3)
+    keep(-3)
     add(3)
     step(1, 1, 1, True)
     add(-3)
@@ -685,7 +700,7 @@
         half(4, 1024, 256), half(4, 1024, 256),
         flat(128, 128), half(384, 256), half(256, 1024), half(256, 256), half(128, 1024),
         flat(2, 128, 256), flat(128, 1024), flat(16, 128), flat(16, 128), flat(128, 16),
-        flat(128, 16), flat(16, 256), flat(128, 1024), flat(8, 128), flat(8, 128),
+        flat(128, 16), flat(16, 256), half(8, 128, 256), flat(128, 1024), flat(8, 128), flat(8, 128),
         flat(8, 128), flat(4, 8, 128), flat(4, 8, 128), half(4, 128, 256),
         half(4, 4, 128, 256), half(4, 4, 128, 256), flat(8, 2, 128, 256),
         half(8, 2, 128, 256), half(8, 2, 128, 256),
@@ -713,6 +728,41 @@
     )(*args)
 
 
+def hand_on_kernel(mixed, state, mixed_out, state_out, mixed_here, state_here, sems, out_sems):
+    pieces = [(mixed, mixed_here, mixed_out)]
+    for q in range(2):
+        for part in range(4):
+            at = (q, pl.ds(256 * part, 256))
+            pieces.append((state.at[at], state_here.at[at], state_out.at[at]))
+    loads = [pltpu.make_async_copy(a, b, sems.at[k]) for k, (a, b, _) in enumerate(pieces)]
+    stores = [pltpu.make_async_copy(b, c, out_sems.at[k]) for k, (_, b, c) in enumerate(pieces)]
+    for copy in loads:
+        copy.start()
+    for load, store in zip(loads, stores):
+        load.wait()
+        store.start()
+    for copy in stores:
+        copy.wait()
+
+
+def hand_on(mixed, state):
+    hbm = pl.BlockSpec(memory_space=pl.ANY)
+    return pl.pallas_call(
+        hand_on_kernel,
+        name="hand_on",
+        out_shape=(
+            jax.ShapeDtypeStruct(mixed.shape, mixed.dtype),
+            jax.ShapeDtypeStruct(state.shape, state.dtype),
+        ),
+        in_specs=[hbm] * 2,
+        out_specs=(hbm,) * 2,
+        scratch_shapes=[
+            pltpu.VMEM(mixed.shape, mixed.dtype), pltpu.VMEM(state.shape, state.dtype),
+            pltpu.SemaphoreType.DMA((9,)), pltpu.SemaphoreType.DMA((9,)),
+        ],
+    )(mixed, state)
+
+
 def on_device(
     tokens, prior_state, conv_inner_state, conv_group_state, gate_weight, inner_weight,
     group_weight, step_weight, conv_inner_weight, conv_inner_bias, conv_group_weight,
@@ -732,6 +782,7 @@
         row(step_bias), row(decay_rate), row(skip_gain), row(norm_gain), out_weight, parents,
         accepted_path, path_length, tree_size,
     )
+    mixed, state = hand_on(mixed, state)
     return mixed, state.reshape(prior_state.shape)
 
 

time: 135 us -> 129 us (0.956)
  local copies, waits for them, and re-layouts: 5.29 us -> 0.6 us
  Pallas kernels: 128 us -> 126 us
    unnamed x2 -> x0, local copies, waits for them, and re-layouts: 4.7 us -> none
    pallas_call x1, Pallas kernels: 128 us -> 124 us  [mixer(): pl.pallas_call(mixer_kernel, name='mixer', out_shape=(shape((128, 512), B...]
    pallas_call x0 -> x1, Pallas kernels: none -> 2.48 us  [hand_on(): pl.pallas_call(hand_on_kernel, name='hand_on', out_shape=(jax.ShapeDtypeS...]
where the time goes in v5:
time: 129 us
  Pallas kernels  126 us (98%)
    pallas_call x1, Pallas kernels, mixer(): pl.pallas_call(mixer_kernel, name='mixer', out_shape=(shape((128, 512), B...  124 us

profile of v5, /device:TPU:16, one launch (start us, length us, event | category | flops | bytes accessed | tf_op | source)
XLA Modules:
  0.0 128.5 jit_solution(9596743434175901490)
XLA Ops:
  0.6 0.7 maximum_convert_fusion
  1.3 0.6 reshape.26.refs_10_
  1.9 123.9 %mixer.1 = (bf16[128,512]{1,0:T(8,128)(2,1)}, f32[2,1024,256]{2,1,0:T(8,128)}) custom-call(bf16[128,512]{1,0:T(8,128)(2,1)} %refs_0_.1, f32[2,1024,256]{2,1,0:T(8,128)} %bitcast.9, bf16[3,2,1024]{2,1,0:T(2,128)(2,1)} %bitcast.11, bf16[3,2,256]{2,1,0:T(2,128)(2,1)} %bitcast.13, bf16[512,1024]{1,0:T(8,128)(2,1)} %refs_4_.1, bf16[512,1024]{1,0:T(8,128)(2,1)} %refs_5_.1, ...), custom_call_target="tpu_custom_call" | custom-call | tf_op jit(solution)/shard_map/mixer/pallas_call | solution.py:718
  125.9 2.5 %hand_on.1 = (bf16[128,512]{1,0:T(8,128)(2,1)}, f32[2,1024,256]{2,1,0:T(8,128)}) custom-call(bf16[128,512]{1,0:T(8,128)(2,1)} %get-tuple-element.6.mixed, f32[2,1024,256]{2,1,0:T(8,128)} %get-tuple-element.7.state), custom_call_target="tpu_custom_call" | custom-call | tf_op jit(solution)/shard_map/hand_on/pallas_call | solution.py:750
